TPU v7x, 256 devices: a whole 4x4x8 slice. The times are simulated.
256 devices in a mesh: dp: 2 (over y_hi), section: 16 (over y_lo, x, core), tensor: 8 (over z).
Axes of the slice: x: 4, y: 4 (y_hi: 2, y_lo: 2; y = y_hi * 2 + y_lo), z: 8, core: 2. Of those that a mesh axis runs over, the one named last changes fastest.
Arguments:
- hidden_in: float32 [32, 4, 16, 8192], P(('dp', 'section'), None, None, 'tensor'), parts along dimension 0
- norm_gain: float32 [32, 2, 8192], P(('dp', 'section'), None, 'tensor'), parts along dimension 0, may hold values from 0.1 to 1.9
- w_qkv: bfloat16 [32, 2, 8192, 1280], P(('dp', 'section'), None, 'tensor'), parts along dimension 0, may hold values from -0.109375 to 0.109375
- w_out: bfloat16 [32, 2, 1024, 8192], P(('dp', 'section'), None, None, 'tensor'), parts along dimension 0, may hold values from -0.1875 to 0.1875
- kv_cache: bfloat16 [32, 4, 4, 512, 256], P(('dp', 'section'), None, None, 'tensor'), parts along dimension 0
- parents: int32 [128, 16], P('dp'), parts along dimension 0, may hold values from 0 to 14, as said below
- lengths: int32 [128], P('dp'), parts along dimension 0, may hold values from 1 to 512, as said below
- assign: int32 [32, 4], P('dp'), parts along dimension 0, may hold values from 0 to 63, as said below
Outputs:
- hidden_out: float32 [32, 4, 16, 8192], P(('dp', 'section'), None, None, 'tensor'), parts along dimension 0
There are 2 independent parts, one for each index of `dp`. A program takes and returns all parts, laid end to end along the dimension named above; each array names one. Nothing has to cross between parts.
Inputs may be any that keep to these rules, and one draw needn't show every extreme that they name: `parents`: node 0 is the root and its entry is 0; node a > 0 has a parent below a; the last node's parent is node 14. `lengths`: some request has length 512. `assign`: every request id appears exactly once.
All inputs are finite; a program needn't handle non-finite values.
Results may differ from a plain program's by a relative error of at most 0.0095.
Values may be sent and summed in bfloat16 or wider, within the bound.
No kernel may reach another device: no remote copies, remote signals or barrier semaphores. Data moves between devices by JAX's collectives and lax.ppermute only.
A program may use at most 64 MiB of HBM per device.

v0:
```python
import jax
import jax.numpy as jnp
from jax import lax
from jax.sharding import PartitionSpec as P

D = 8192


epsilon = 1e-05
lowest = -1e30


def joined(value, axis, join):
    pieces = jax.tree.map(lambda part: lax.all_gather(part, axis), value)
    head = jax.tree.map(lambda part: part[0], pieces)
    tail = jax.tree.map(lambda part: part[1:], pieces)
    total, _ = lax.scan(lambda total, section: (join(total, section), None), head, tail)
    return total


def shifted(value, axis, steps):
    count = lax.axis_size(axis)
    pairs = [(source, (source + steps) % count) for source in range(count)]
    return lax.ppermute(value, axis, pairs)


def ancestors(parent_rows):
    node_count = parent_rows.shape[1]
    identity = jnp.eye(node_count, dtype=jnp.float32)
    ancestor_rows = [jnp.broadcast_to(identity[0], (parent_rows.shape[0], node_count))]
    for node_index in range(1, node_count):
        onehot = (
            parent_rows[:, node_index][:, None] == jnp.arange(node_index, dtype=jnp.int32)[None, :]
        ).astype(jnp.float32)
        earlier = jnp.stack(ancestor_rows, axis=1)
        ancestor_rows.append(jnp.einsum("rn,rnt->rt", onehot, earlier) + identity[node_index])
    return jnp.stack(ancestor_rows, axis=1) > 0.5


def partial_softmax(scores, valid, values, pattern):
    masked = jnp.where(valid, scores, lowest)
    row_max = jnp.max(masked, axis=-1)
    weights = jnp.exp(masked - row_max[..., None]) * valid.astype(jnp.float32)
    row_sum = jnp.sum(weights, axis=-1)
    weighted = jnp.einsum(
        pattern, weights.astype(jnp.bfloat16), values, preferred_element_type=jnp.float32
    )
    return (row_max, row_sum, weighted)


def combine(left_part, right_part):
    joint_max = jnp.maximum(left_part[0], right_part[0])
    scale_left = jnp.exp(left_part[0] - joint_max)
    scale_right = jnp.exp(right_part[0] - joint_max)
    row_sum = left_part[1] * scale_left + right_part[1] * scale_right
    weighted = left_part[2] * scale_left[..., None] + right_part[2] * scale_right[..., None]
    return (joint_max, row_sum, weighted)


def tree_part(queries, tree_keys, tree_values, visible, scaling):
    scores = (
        jnp.einsum("rthe,rse->rths", queries, tree_keys, preferred_element_type=jnp.float32)
        * scaling
    )
    return partial_softmax(scores, visible[:, :, None, :], tree_values, "rths,rse->rthe")


def body(hidden_in, norm_gain, w_qkv, w_out, kv_cache, parents, lengths, assign):
    section_index = lax.axis_index("section")
    section_count = lax.axis_size("section")
    tensor_index = lax.axis_index("tensor")
    head_size = kv_cache.shape[-1] // 2
    heads_total = w_out.shape[2] // head_size
    local_ctx = kv_cache.shape[3]
    requests = parents.shape[0]
    scaling = head_size ** (-0.5)
    state = hidden_in[0]
    batch_rows, tree_size, local_width = state.shape
    positions = tensor_index * local_ctx + jnp.arange(local_ctx, dtype=jnp.int32)
    for step_index in range(kv_cache.shape[1]):
        held_batch = (section_index - step_index) % section_count
        which = (section_index < step_index).astype(jnp.int32)
        request_ids = lax.dynamic_index_in_dim(assign, held_batch, 0, keepdims=False)
        select = (request_ids[:, None] == jnp.arange(requests, dtype=jnp.int32)[None, :]).astype(
            jnp.float32
        )
        length_rows = jnp.dot(
            select, lengths.astype(jnp.float32), precision=lax.Precision.HIGHEST
        ).astype(jnp.int32)
        parent_rows = jnp.dot(
            select, parents.astype(jnp.float32), precision=lax.Precision.HIGHEST
        ).astype(jnp.int32)
        visible = ancestors(parent_rows)
        gain_row = lax.dynamic_index_in_dim(norm_gain[0], which, 0, keepdims=False)
        weight_in = lax.dynamic_index_in_dim(w_qkv[0], which, 0, keepdims=False)
        weight_out = lax.dynamic_index_in_dim(w_out[0], which, 0, keepdims=False)
        square_sum = lax.psum(jnp.sum(state * state, axis=-1), "tensor")
        factor = lax.rsqrt(square_sum / D + epsilon)
        normed = (state * factor[..., None] * gain_row).astype(jnp.bfloat16)
        partial_proj = jnp.dot(
            normed.reshape(-1, local_width), weight_in, preferred_element_type=jnp.float32
        )
        projected = lax.psum(partial_proj, "tensor")
        projected = projected.astype(jnp.bfloat16).reshape(
            batch_rows, tree_size, heads_total + 2, head_size
        )
        queries = projected[:, :, :heads_total]
        tree_keys = projected[:, :, heads_total]
        tree_values = projected[:, :, heads_total + 1]
        cache_now = kv_cache[0, step_index]
        cache_keys = cache_now[..., :head_size]
        cache_values = cache_now[..., head_size:]
        live_keys = positions[None, :] < length_rows[:, None]
        cache_scores = (
            jnp.einsum("rthe,rce->rthc", queries, cache_keys, preferred_element_type=jnp.float32)
            * scaling
        )
        cache_result = partial_softmax(
            cache_scores, live_keys[:, None, None, :], cache_values, "rthc,rce->rthe"
        )
        merged = joined(cache_result, "tensor", combine)
        combined = combine(merged, tree_part(queries, tree_keys, tree_values, visible, scaling))
        attended = (combined[2] / combined[1][..., None]).astype(jnp.bfloat16)
        attended = attended.reshape(batch_rows * tree_size, heads_total * head_size)
        update = jnp.dot(attended, weight_out, preferred_element_type=jnp.float32)
        state = state + update.reshape(state.shape)
        state = shifted(state, "section", 1)
    return state[None]


def solution(mesh):
    in_specs = (
        P(("dp", "section"), None, None, "tensor"),
        P(("dp", "section"), None, "tensor"),
        P(("dp", "section"), None, "tensor", None),
        P(("dp", "section"), None, None, "tensor"),
        P(("dp", "section"), None, None, "tensor", None),
        P("dp", None),
        P("dp"),
        P("dp", None),
    )
    out_specs = P(("dp", "section"), None, None, "tensor")
    return jax.shard_map(body, mesh=mesh, in_specs=in_specs, out_specs=out_specs, check_vma=False)
```

profile of v0, /device:TPU:16, one launch (start us, length us, event | category | flops | bytes accessed | tf_op | source)
XLA Modules:
  0.0 507.5 jit_solution(10655327356138790066)
XLA Ops:
  8.8 20.0 %psum.56 = f32[4,16]{1,0:T(4,128)S(1)} all-reduce(f32[4,16]{1,0:T(4,128)S(1)} %fusion.72), channel_id=1, replica_groups=mesh['dp'=2,'section'=16,'tensor'=8] {'tensor'}, use_global_device_ids=true, to_apply=%region_1.2 | all-reduce | flops 64 | bytes 512 | tf_op jit(solution)/shard_map/psum | solution.py:97
  33.0 30.7 %all-reduce.4 = bf16[64,1280]{1,0:T(8,128)(2,1)S(1)} all-reduce(f32[64,1280]{1,0:T(8,128)S(1)} %fusion.18), channel_id=1, replica_groups=mesh['dp'=2,'section'=16,'tensor'=8] {'tensor'}, use_global_device_ids=true, to_apply=%region_2.3 | all-reduce | flops 81920 | bytes 491520 | tf_op jit(solution)/shard_map/psum | solution.py:103
  66.6 24.7 %all-gather = f32[32,16,8]{1,2,0:T(8,128)S(1)} all-gather(f32[4,16,8]{1,2,0:T(8,128)S(1)} %copy.125), channel_id=2, replica_groups=mesh['dp'=2,'section'=16,'tensor'=8] {'tensor'}, dimensions={0}, use_global_device_ids=true | all-gather | bytes 18432 | tf_op jit(solution)/shard_map/all_gather | solution.py:14
  91.4 24.6 %all-gather.1 = f32[32,16,8]{1,2,0:T(8,128)S(1)} all-gather(f32[4,16,8]{1,2,0:T(8,128)S(1)} %copy.126), channel_id=3, replica_groups=mesh['dp'=2,'section'=16,'tensor'=8] {'tensor'}, dimensions={0}, use_global_device_ids=true | all-gather | bytes 18432 | tf_op jit(solution)/shard_map/all_gather | solution.py:14
  135.3 3.2 while.56
  141.7 7.9 %collective-permute-done = f32[4,16,1024]{2,1,0:T(8,128)S(1)} collective-permute-done((f32[4,16,1024]{2,1,0:T(8,128)S(1)}, f32[4,16,1024]{2,1,0:T(8,128)S(1)}, u32[]{:S(2)}, u32[]{:S(2)}) %collective-permute-start) | collective-permute-done | bytes 262176 | tf_op jit(solution)/shard_map/ppermute | solution.py:24
  149.7 16.2 %psum.58 = f32[4,16]{1,0:T(4,128)S(1)} all-reduce(f32[4,16]{1,0:T(4,128)S(1)} %multiply_reduce_fusion.2), channel_id=1, replica_groups=mesh['dp'=2,'section'=16,'tensor'=8] {'tensor'}, use_global_device_ids=true, to_apply=%region_10.11 | all-reduce | flops 64 | bytes 512 | tf_op jit(solution)/shard_map/psum | solution.py:97
  168.3 30.6 %all-reduce.5 = bf16[64,1280]{1,0:T(8,128)(2,1)S(1)} all-reduce(f32[64,1280]{1,0:T(8,128)S(1)} %fusion.16), channel_id=1, replica_groups=mesh['dp'=2,'section'=16,'tensor'=8] {'tensor'}, use_global_device_ids=true, to_apply=%region_11.12 | all-reduce | flops 81920 | bytes 491520 | tf_op jit(solution)/shard_map/psum | solution.py:103
  200.6 24.7 %all-gather.3 = f32[32,16,8]{1,2,0:T(8,128)S(1)} all-gather(f32[4,16,8]{1,2,0:T(8,128)S(1)} %copy.253), channel_id=5, replica_groups=mesh['dp'=2,'section'=16,'tensor'=8] {'tensor'}, dimensions={0}, use_global_device_ids=true | all-gather | bytes 18432 | tf_op jit(solution)/shard_map/all_gather | solution.py:14
  225.6 24.8 %all-gather.4 = f32[32,16,8]{1,2,0:T(8,128)S(1)} all-gather(f32[4,16,8]{1,2,0:T(8,128)S(1)} %copy.254), channel_id=6, replica_groups=mesh['dp'=2,'section'=16,'tensor'=8] {'tensor'}, dimensions={0}, use_global_device_ids=true | all-gather | bytes 18432 | tf_op jit(solution)/shard_map/all_gather | solution.py:14
  252.8 3.2 while.57
  258.9 7.9 %collective-permute-done.1 = f32[4,16,1024]{2,1,0:T(8,128)S(1)} collective-permute-done((f32[4,16,1024]{2,1,0:T(8,128)S(1)}, f32[4,16,1024]{2,1,0:T(8,128)S(1)}, u32[]{:S(2)}, u32[]{:S(2)}) %collective-permute-start.1) | collective-permute-done | bytes 262176 | tf_op jit(solution)/shard_map/ppermute | solution.py:24
  266.8 16.0 %psum.60 = f32[4,16]{1,0:T(4,128)S(1)} all-reduce(f32[4,16]{1,0:T(4,128)S(1)} %multiply_reduce_fusion.1), channel_id=1, replica_groups=mesh['dp'=2,'section'=16,'tensor'=8] {'tensor'}, use_global_device_ids=true, to_apply=%region_19.20 | all-reduce | flops 64 | bytes 512 | tf_op jit(solution)/shard_map/psum | solution.py:97
  285.2 31.1 %all-reduce.6 = bf16[64,1280]{1,0:T(8,128)(2,1)S(1)} all-reduce(f32[64,1280]{1,0:T(8,128)S(1)} %fusion.14), channel_id=1, replica_groups=mesh['dp'=2,'section'=16,'tensor'=8] {'tensor'}, use_global_device_ids=true, to_apply=%region_20.21 | all-reduce | flops 81920 | bytes 491520 | tf_op jit(solution)/shard_map/psum | solution.py:103
  317.9 24.6 %all-gather.6 = f32[32,16,8]{1,2,0:T(8,128)S(1)} all-gather(f32[4,16,8]{1,2,0:T(8,128)S(1)} %copy.381), channel_id=8, replica_groups=mesh['dp'=2,'section'=16,'tensor'=8] {'tensor'}, dimensions={0}, use_global_device_ids=true | all-gather | bytes 18432 | tf_op jit(solution)/shard_map/all_gather | solution.py:14
  342.9 24.6 %all-gather.7 = f32[32,16,8]{1,2,0:T(8,128)S(1)} all-gather(f32[4,16,8]{1,2,0:T(8,128)S(1)} %copy.382), channel_id=9, replica_groups=mesh['dp'=2,'section'=16,'tensor'=8] {'tensor'}, dimensions={0}, use_global_device_ids=true | all-gather | bytes 18432 | tf_op jit(solution)/shard_map/all_gather | solution.py:14
  369.9 3.2 while.58
  375.9 7.9 %collective-permute-done.2 = f32[4,16,1024]{2,1,0:T(8,128)S(1)} collective-permute-done((f32[4,16,1024]{2,1,0:T(8,128)S(1)}, f32[4,16,1024]{2,1,0:T(8,128)S(1)}, u32[]{:S(2)}, u32[]{:S(2)}) %collective-permute-start.2) | collective-permute-done | bytes 262176 | tf_op jit(solution)/shard_map/ppermute | solution.py:24
  383.9 15.7 %psum.62 = f32[4,16]{1,0:T(4,128)S(1)} all-reduce(f32[4,16]{1,0:T(4,128)S(1)} %multiply_reduce_fusion), channel_id=1, replica_groups=mesh['dp'=2,'section'=16,'tensor'=8] {'tensor'}, use_global_device_ids=true, to_apply=%region_28.29 | all-reduce | flops 64 | bytes 512 | tf_op jit(solution)/shard_map/psum | solution.py:97
  402.0 30.8 %all-reduce.7 = bf16[64,1280]{1,0:T(8,128)(2,1)S(1)} all-reduce(f32[64,1280]{1,0:T(8,128)S(1)} %fusion.12), channel_id=1, replica_groups=mesh['dp'=2,'section'=16,'tensor'=8] {'tensor'}, use_global_device_ids=true, to_apply=%region_29.30 | all-reduce | flops 81920 | bytes 491520 | tf_op jit(solution)/shard_map/psum | solution.py:103
  434.4 24.6 %all-gather.9 = f32[32,16,8]{1,2,0:T(8,128)S(1)} all-gather(f32[4,16,8]{1,2,0:T(8,128)S(1)} %copy.509), channel_id=11, replica_groups=mesh['dp'=2,'section'=16,'tensor'=8] {'tensor'}, dimensions={0}, use_global_device_ids=true | all-gather | bytes 18432 | tf_op jit(solution)/shard_map/all_gather | solution.py:14
  459.3 24.6 %all-gather.10 = f32[32,16,8]{1,2,0:T(8,128)S(1)} all-gather(f32[4,16,8]{1,2,0:T(8,128)S(1)} %copy.510), channel_id=12, replica_groups=mesh['dp'=2,'section'=16,'tensor'=8] {'tensor'}, dimensions={0}, use_global_device_ids=true | all-gather | bytes 18432 | tf_op jit(solution)/shard_map/all_gather | solution.py:14
  486.3 3.2 while.59
  492.4 7.9 %collective-permute-done.3 = f32[4,16,1024]{2,1,0:T(8,128)S(1)} collective-permute-done((f32[4,16,1024]{2,1,0:T(8,128)S(1)}, f32[4,16,1024]{2,1,0:T(8,128)S(1)}, u32[]{:S(2)}, u32[]{:S(2)}) %collective-permute-start.3) | collective-permute-done | bytes 262176 | tf_op jit(solution)/shard_map/ppermute | solution.py:24
  (460 shorter events, 73.1 us)
Async XLA Ops:
  6.5 127.1 %all-gather.17.cloned.1.call-start = ((), (), s32[]{:S(2)}) async-start(), calls=%async_computation | async-start | bytes 2359296 | tf_op jit(solution)/shard_map/all_gather | solution.py:14
  7.7 56.2 %copy-start.3 = (s32[16,4]{0,1:T(4,128)S(1)}, s32[16,4]{0,1:T(4,128)}, u32[]{:S(2)}) copy-start(s32[16,4]{0,1:T(4,128)} %param.23) | copy-start | bytes 772
  7.7 56.4 %copy-start.5 = (s32[64]{0:T(128)S(1)}, s32[64]{0:T(128)}, u32[]{:S(2)}) copy-start(s32[64]{0:T(128)} %param.22) | copy-start | bytes 772
  33.0 83.0 %copy-start.4 = (s32[64,16]{0,1:T(8,128)S(1)}, s32[64,16]{0,1:T(8,128)}, u32[]{:S(2)}) copy-start(s32[64,16]{0,1:T(8,128)} %param.21) | copy-start | bytes 12292
  66.2 185.0 %all-gather.19.cloned.1.call-start = ((), (), s32[]{:S(2)}) async-start(), calls=%async_computation.1 | async-start | bytes 2359296 | tf_op jit(solution)/shard_map/all_gather | solution.py:14
  91.3 41.9 %copy-start.1 = (f32[32,16,8]{1,2,0:T(8,128)}, f32[32,16,8]{1,2,0:T(8,128)S(1)}, u32[]{:S(2)}) copy-start(f32[32,16,8]{1,2,0:T(8,128)S(1)} %all-gather) | copy-start | bytes 49156
  116.0 17.6 %copy-start.2 = (f32[32,16,8]{1,2,0:T(8,128)}, f32[32,16,8]{1,2,0:T(8,128)S(1)}, u32[]{:S(2)}) copy-start(f32[32,16,8]{1,2,0:T(8,128)S(1)} %all-gather.1) | copy-start | bytes 49156
  133.2 1.6 slice-start.4
  133.7 1.1 slice-start.5
  133.7 1.7 slice-start.1
  138.5 1.0 copy-start
  141.6 8.0 %collective-permute-start = (f32[4,16,1024]{2,1,0:T(8,128)S(1)}, f32[4,16,1024]{2,1,0:T(8,128)S(1)}, u32[]{:S(2)}, u32[]{:S(2)}) collective-permute-start(f32[4,16,1024]{2,1,0:T(8,128)S(1)} %fusion.36), channel_id=1, source_target_pairs={{0,8},{8,16},{16,24},{24,32},{32,40},{40,48},{48,56},{56,64},{64,7... | collective-permute-start | bytes 786440 | tf_op jit(solution)/shard_map/ppermute | solution.py:24
  200.3 167.9 %all-gather.21.cloned.1.call-start = ((), (), s32[]{:S(2)}) async-start(), calls=%async_computation.2 | async-start | bytes 2359296 | tf_op jit(solution)/shard_map/all_gather | solution.py:14
  251.2 1.6 slice-start.2
  258.8 8.0 %collective-permute-start.1 = (f32[4,16,1024]{2,1,0:T(8,128)S(1)}, f32[4,16,1024]{2,1,0:T(8,128)S(1)}, u32[]{:S(2)}, u32[]{:S(2)}) collective-permute-start(f32[4,16,1024]{2,1,0:T(8,128)S(1)} %fusion.39), channel_id=1, source_target_pairs={{0,8},{8,16},{16,24},{24,32},{32,40},{40,48},{48,56},{56,64},{64,7... | collective-permute-start | bytes 786440 | tf_op jit(solution)/shard_map/ppermute | solution.py:24
  317.7 167.0 %all-gather.23.cloned.1.call-start = ((), (), s32[]{:S(2)}) async-start(), calls=%async_computation.3 | async-start | bytes 2359296 | tf_op jit(solution)/shard_map/all_gather | solution.py:14
  368.3 1.6 slice-start.3
  375.8 8.0 %collective-permute-start.2 = (f32[4,16,1024]{2,1,0:T(8,128)S(1)}, f32[4,16,1024]{2,1,0:T(8,128)S(1)}, u32[]{:S(2)}, u32[]{:S(2)}) collective-permute-start(f32[4,16,1024]{2,1,0:T(8,128)S(1)} %fusion.42), channel_id=1, source_target_pairs={{0,8},{8,16},{16,24},{24,32},{32,40},{40,48},{48,56},{56,64},{64,7... | collective-permute-start | bytes 786440 | tf_op jit(solution)/shard_map/ppermute | solution.py:24
  484.7 1.6 slice-start
  492.3 8.0 %collective-permute-start.3 = (f32[4,16,1024]{2,1,0:T(8,128)S(1)}, f32[4,16,1024]{2,1,0:T(8,128)S(1)}, u32[]{:S(2)}, u32[]{:S(2)}) collective-permute-start(f32[4,16,1024]{2,1,0:T(8,128)S(1)} %fusion.45), channel_id=1, source_target_pairs={{0,8},{8,16},{16,24},{24,32},{32,40},{40,48},{48,56},{56,64},{64,7... | collective-permute-start | bytes 786440 | tf_op jit(solution)/shard_map/ppermute | solution.py:24
Sparse Core Ops, SparseCore 0:
  66.3 40.3 all-gather.16
  200.5 38.8 all-gather.18
  317.8 37.3 all-gather.20
  434.3 38.1 all-gather.22
where the time goes:
time: 509 us; the launch traced here: 508 us
  blocking collectives  388 us (76%)
  matrix products  33.4 us (7%)
  waiting for transfers between devices  31.6 us (6%)
  local copies, waits for them, and re-layouts  21.3 us (4%)
  other arithmetic  17.8 us (3%)
  between operations  13.9 us (3%)
    all_gather x8, blocking collectives, joined(): pieces = jax.tree.map(lambda part: lax.all_gather(part, axis), value)  197 us
    psum x4, blocking collectives, body(): projected = lax.psum(partial_proj, 'tensor')  123 us
    psum x4, blocking collectives, body(): square_sum = lax.psum(jnp.sum(state * state, axis=-1), 'tensor')  67.9 us
    ppermute x4, waiting for transfers between devices, shifted(): return lax.ppermute(value, axis, pairs)  31.6 us
  transfers between devices with their start and end apart: 8, of which 4 were waited for; matrix products, arithmetic and copies ran while one was open for 4% of the time, Pallas kernels for 0%

commit v1 on v0

v1 whole, which is shorter than its diff:
```python
import functools

import jax
import jax.numpy as jnp
from jax import lax
from jax.experimental import pallas as pl
from jax.experimental.pallas import tpu as pltpu
from jax.sharding import PartitionSpec as P

bf16 = jnp.bfloat16
f32 = jnp.float32

D = 8192
epsilon = 1e-05
lowest = -1e30
largest = 3.3e38

TREE = 16
HEAD = 128
BOTH = 2 * HEAD
HALF = 512
MIX = 768
PIECE = 896
CHUNKS = 8
VMEM_LIMIT = 16 * 1024 * 1024

VMEM = pl.BlockSpec(memory_space=pltpu.VMEM)
FAR = pl.BlockSpec(memory_space=pltpu.HBM)
PARAMS = pltpu.CompilerParams(vmem_limit_bytes=VMEM_LIMIT)


def layer_of(step):
    return (lax.axis_index("section") < step).astype(jnp.int32)


def loads(source, target, sems):
    count = sems.shape[0]
    rows = target.shape[0] // count
    return [
        pltpu.make_async_copy(
            source.at[pl.ds(part * rows, rows), :],
            target.at[pl.ds(part * rows, rows), :],
            sems.at[part],
        )
        for part in range(count)
    ]


def write_pieces(out_ref, raw, state):
    square = jnp.sum(state * state, axis=-1, keepdims=True)
    high = jnp.minimum(square, largest).astype(bf16)
    low = (square - high.astype(f32)).astype(bf16)
    lane = lax.broadcasted_iota(jnp.int32, (state.shape[0], HEAD), 1)
    pair = jnp.where(lane < HEAD // 2, high.astype(f32), low.astype(f32)).astype(bf16)
    raw = raw.astype(bf16)
    for slot in range(out_ref.shape[0] // 2):
        here = slice(slot * TREE, (slot + 1) * TREE)
        for half in range(2):
            out_ref[2 * slot + half, :, :HALF] = raw[here, half * HALF : (half + 1) * HALF]
            out_ref[2 * slot + half, :, HALF:MIX] = raw[here, 2 * HALF :]
            out_ref[2 * slot + half, :, MIX:PIECE] = pair[here]


def write_cache(out_ref, cache_ref, step):
    for slot in range(cache_ref.shape[1]):
        for chunk in range(cache_ref.shape[2] // TREE):
            block = cache_ref[step, slot, chunk * TREE : (chunk + 1) * TREE, :]
            start = PIECE + chunk * BOTH
            for half in range(2):
                out_ref[2 * slot + half, :, start : start + BOTH] = block


def first_kernel(
    assign_far, parents_far, lengths_far, state_far, gain_far, weight_far, cache_far,
    out_ref, state_ref, table_ref, gain_ref, weight_ref, cache_ref,
    assign_ref, parents_ref, lengths_ref, rows, sems, more,
):
    layers = weight_ref.shape[0]
    weight_copies = [
        loads(weight_far.at[0, layer], weight_ref.at[layer], sems.at[layer])
        for layer in range(layers)
    ]
    other = [
        pltpu.make_async_copy(source, target, more.at[index])
        for index, (source, target) in enumerate(
            (
                (assign_far, assign_ref),
                (parents_far, parents_ref),
                (lengths_far, lengths_ref),
                (state_far.at[0], state_ref),
                (gain_far.at[0], gain_ref),
                (cache_far.at[0], cache_ref),
            )
        )
    ]
    for copy in other[:5] + weight_copies[0] + other[5:] + sum(weight_copies[1:], []):
        copy.start()
    for copy in other[:3]:
        copy.wait()
    batches = assign_ref.shape[1]
    section = lax.axis_index("section")
    slot = lax.axis_index("tensor") // 2
    lane = lax.broadcasted_iota(jnp.int32, (1, HEAD), 1)
    steps = range(table_ref.shape[0])
    held = [lax.rem(section - step + batches, batches) for step in steps]
    request = [assign_ref[slot, held[step]] for step in steps]
    for step in steps:
        rows[step, pl.ds(0, 1), :] = jnp.where(lane == 0, 1.0, 0.0)
    for node in range(1, TREE):
        parents = [parents_ref[node, request[step]] for step in steps]
        above = [rows[step, pl.ds(parents[step], 1), :] for step in steps]
        for step in steps:
            rows[step, pl.ds(node, 1), :] = jnp.where(lane == node, 1.0, above[step])
    for step in steps:
        live = lengths_ref[request[step]].astype(f32)
        table_ref[step] = jnp.where(lane < TREE, rows[step], live)
    other[3].wait()
    other[4].wait()
    slots, tree, width = state_ref.shape
    state = state_ref[...].reshape(slots * tree, width)
    scaled = (state * gain_ref[0:1, :]).astype(bf16)
    depth = width // len(weight_copies[0])
    raw = jnp.zeros((slots * tree, weight_ref.shape[2]), f32)
    for part, copy in enumerate(weight_copies[0]):
        copy.wait()
        span = slice(part * depth, (part + 1) * depth)
        raw = raw + jnp.dot(scaled[:, span], weight_ref[0, span, :], preferred_element_type=f32)
    write_pieces(out_ref, raw, state)
    other[5].wait()
    write_cache(out_ref, cache_ref, 0)
    for copy in sum(weight_copies[1:], []):
        copy.wait()


def first(assign, parents, lengths, hidden, gain, weight, cache):
    _, slots, tree, width = hidden.shape
    steps, _, span = cache.shape[1:4]
    return pl.pallas_call(
        first_kernel,
        out_shape=(
            jax.ShapeDtypeStruct((2 * slots, TREE, PIECE + span // TREE * BOTH), bf16),
            pltpu.VMEM((slots, tree, width), f32),
            pltpu.VMEM((steps, TREE, HEAD), f32),
            pltpu.VMEM(gain.shape[1:], f32),
            pltpu.VMEM(weight.shape[1:], bf16),
            pltpu.VMEM(cache.shape[1:], bf16),
        ),
        in_specs=[FAR] * 7,
        out_specs=(VMEM,) * 6,
        scratch_shapes=[
            pltpu.SMEM(assign.shape[::-1], jnp.int32),
            pltpu.SMEM(parents.shape[::-1], jnp.int32),
            pltpu.SMEM(lengths.shape, jnp.int32),
            pltpu.VMEM((steps, TREE, HEAD), f32),
            pltpu.SemaphoreType.DMA((weight.shape[1], CHUNKS)),
            pltpu.SemaphoreType.DMA((6,)),
        ],
        compiler_params=PARAMS,
    )(*(far(value) for value in (assign.T, parents.T, lengths, hidden, gain, weight, cache)))


def project_kernel(state_ref, gain_ref, weight_ref, cache_ref, out_ref, *, step):
    slots, tree, width = state_ref.shape
    state = state_ref[...].reshape(slots * tree, width)
    which = layer_of(step)
    scaled = (state * gain_ref[pl.ds(which, 1), :]).astype(bf16)
    raw = jnp.dot(scaled, weight_ref[which], preferred_element_type=f32)
    write_pieces(out_ref, raw, state)
    write_cache(out_ref, cache_ref, step)


def project(state, gain, weight, cache, step):
    slots, span = cache.shape[1:3]
    return pl.pallas_call(
        functools.partial(project_kernel, step=step),
        out_shape=jax.ShapeDtypeStruct((2 * slots, TREE, PIECE + span // TREE * BOTH), bf16),
        in_specs=[VMEM] * 4,
        out_specs=VMEM,
        compiler_params=PARAMS,
    )(state, gain, weight, cache)


def attend_kernel(got_ref, table_ref, *refs, step):
    if step:
        (out_ref,) = refs
        copies = []
    else:
        weight_far, out_ref, weight_ref, sems = refs
        copies = sum(
            (
                loads(weight_far.at[0, layer], weight_ref.at[layer], sems.at[layer])
                for layer in range(weight_ref.shape[0])
            ),
            [],
        )
    for copy in copies:
        copy.start()
    total = jnp.sum(got_ref[:, :, :PIECE].astype(f32), axis=0)
    square = total[:, MIX : MIX + 1] + total[:, MIX + HEAD // 2 : MIX + HEAD // 2 + 1]
    factor = lax.rsqrt(square / D + epsilon)
    projected = (total[:, :MIX] * factor).astype(bf16)
    heads = HALF // HEAD
    queries = jnp.concatenate(
        [projected[:, h * HEAD : (h + 1) * HEAD] for h in range(heads)], axis=0
    )
    tree_keys = projected[:, HALF : HALF + HEAD]
    tree_values = projected[:, HALF + HEAD :]
    keys, values = (
        jnp.concatenate(
            [
                got_ref[piece, :, start + side : start + side + HEAD]
                for piece in range(got_ref.shape[0])
                for start in range(PIECE, got_ref.shape[2], BOTH)
            ],
            axis=0,
        )
        for side in (0, HEAD)
    )
    contract = (((1,), (1,)), ((), ()))
    scaling = HEAD ** (-0.5)
    scores = lax.dot_general(queries, keys, contract, preferred_element_type=f32)
    tree_scores = lax.dot_general(queries, tree_keys, contract, preferred_element_type=f32)
    position = lax.broadcasted_iota(jnp.int32, scores.shape, 1)
    table = table_ref[step]
    live = table[0:1, TREE : TREE + 1].astype(jnp.int32)
    visible = jnp.concatenate([table[:, :TREE]] * heads, axis=0) > 0.5
    scores = jnp.where(position < live, scores * scaling, lowest)
    tree_scores = jnp.where(visible, tree_scores * scaling, lowest)
    row_max = jnp.maximum(
        jnp.max(scores, axis=-1, keepdims=True), jnp.max(tree_scores, axis=-1, keepdims=True)
    )
    weights = jnp.exp(scores - row_max)
    tree_weights = jnp.exp(tree_scores - row_max)
    row_sum = jnp.sum(weights, axis=-1, keepdims=True) + jnp.sum(
        tree_weights, axis=-1, keepdims=True
    )
    weighted = jnp.dot(weights.astype(bf16), values, preferred_element_type=f32)
    weighted = weighted + jnp.dot(
        tree_weights.astype(bf16), tree_values, preferred_element_type=f32
    )
    attended = (weighted / row_sum).astype(bf16)
    for h in range(heads):
        part = attended[h * TREE : (h + 1) * TREE]
        for piece in range(out_ref.shape[0]):
            out_ref[piece, :, h * HEAD : (h + 1) * HEAD] = part
    for copy in copies:
        copy.wait()


def attend(got, table, step, weight=None):
    out_shape = (jax.ShapeDtypeStruct((got.shape[0], TREE, HALF), bf16),)
    extra, scratch = (), []
    if weight is not None:
        out_shape += (pltpu.VMEM(weight.shape[1:], bf16),)
        extra = (far(weight),)
        scratch = [pltpu.SemaphoreType.DMA((weight.shape[1], CHUNKS))]
    return pl.pallas_call(
        functools.partial(attend_kernel, step=step),
        out_shape=out_shape,
        in_specs=[VMEM] * 2 + [FAR] * len(extra),
        out_specs=(VMEM,) * len(out_shape),
        scratch_shapes=scratch,
        compiler_params=PARAMS,
    )(got, table, *extra)


def update_kernel(state_ref, got_ref, weight_ref, out_ref, *, step):
    slots = got_ref.shape[0] // 2
    attended = jnp.concatenate(
        [jnp.concatenate([got_ref[2 * s], got_ref[2 * s + 1]], axis=1) for s in range(slots)],
        axis=0,
    )
    delta = jnp.dot(attended, weight_ref[layer_of(step)], preferred_element_type=f32)
    out_ref[...] = state_ref[...] + delta.reshape(out_ref.shape)


def update(state, got, weight, step):
    return pl.pallas_call(
        functools.partial(update_kernel, step=step),
        out_shape=jax.ShapeDtypeStruct(state.shape, f32),
        in_specs=[VMEM] * 3,
        out_specs=VMEM,
        compiler_params=PARAMS,
    )(state, got, weight)


def exchange(value):
    return lax.all_to_all(value, "tensor", 0, 0, tiled=True)


def far(value):
    return pltpu.with_memory_space_constraint(value, pltpu.HBM)


def body(hidden_in, norm_gain, w_qkv, w_out, kv_cache, parents, lengths, assign):
    sections = lax.axis_size("section")
    ring = [(s, (s + 1) % sections) for s in range(sections)]
    pieces, state, table, gain, weight_in, cache = first(
        assign, parents, lengths, hidden_in, norm_gain, w_qkv, kv_cache
    )
    weight_out = None
    for step in range(kv_cache.shape[1]):
        if step:
            pieces = project(state, gain, weight_in, cache, step)
        got = exchange(pieces)
        if step:
            (spread,) = attend(got, table, step)
        else:
            spread, weight_out = attend(got, table, step, w_out)
        state = update(state, exchange(spread), weight_out, step)
        state = lax.ppermute(state, "section", ring)
    return state[None]


def solution(mesh):
    in_specs = (
        P(("dp", "section"), None, None, "tensor"),
        P(("dp", "section"), None, "tensor"),
        P(("dp", "section"), None, "tensor", None),
        P(("dp", "section"), None, None, "tensor"),
        P(("dp", "section"), None, None, "tensor", None),
        P("dp", None),
        P("dp"),
        P("dp", None),
    )
    out_specs = P(("dp", "section"), None, None, "tensor")
    return jax.shard_map(body, mesh=mesh, in_specs=in_specs, out_specs=out_specs, check_vma=False)
```

time: 509 us -> 165 us (0.32)
  blocking collectives: 388 us -> 121 us
  matrix products: 33.4 us -> 0 us
  local copies, waits for them, and re-layouts: 21.3 us -> 0.7 us
  other arithmetic: 17.8 us -> 0 us
  between operations: 13.9 us -> 0.13 us
  Pallas kernels: 0 us -> 11.2 us
    all_gather x8 -> x0, blocking collectives: 197 us -> none  [joined(): pieces = jax.tree.map(lambda part: lax.all_gather(part, axis), value)]
    psum x8 -> x0, blocking collectives: 191 us -> none  [the longest x4 123 us: body(): projected = lax.psum(partial_proj, 'tensor')]
    all_to_all x0 -> x8, blocking collectives: none -> 121 us  [exchange(): return lax.all_to_all(value, 'tensor', 0, 0, tiled=True)]
    dot_general x88 -> x0, matrix products: 33.4 us -> none  [the longest x4 9.23 us: body(): jnp.dot(normed.reshape(-1, local_width), weight_in, preferred_element_typ...]
    pallas_call x0 -> x12, Pallas kernels: none -> 11.2 us  [the longest x4 4.11 us: attend(): pl.pallas_call(functools.partial(attend_kernel, step=step), out_shape=out...]
    add x76 -> x0, other arithmetic: 8.36 us -> none  [the longest x28 7.51 us: combine(): left_part[2] * scale_left[..., None]]
    slice x38 -> x0, local copies, waits for them, and re-layouts: 8.26 us -> none  [the longest x12 4.45 us: joined(): head = jax.tree.map(lambda part: part[0], pieces)]
  transfers between devices with their start and end apart: 8 -> 4, of which waited for: 4 -> 4; matrix products, arithmetic and copies ran while one was open for 4% -> 0% of each run, Pallas kernels for 0% -> 0%
where the time goes in v1:
time: 165 us; the launch traced here: 164 us
  blocking collectives  121 us (73%)
  waiting for transfers between devices  31.6 us (19%)
  Pallas kernels  11.2 us (7%)
    all_to_all x8, blocking collectives, exchange(): return lax.all_to_all(value, 'tensor', 0, 0, tiled=True)  121 us
    ppermute x4, waiting for transfers between devices, body(): state = lax.ppermute(state, 'section', ring)  31.6 us
    pallas_call x4, Pallas kernels, attend(): pl.pallas_call(functools.partial(attend_kernel, step=step), out_shape=out...  4.11 us
    pallas_call x1, Pallas kernels, first(): pl.pallas_call(first_kernel, out_shape=(jax.ShapeDtypeStruct((2 * slots,...  3.37 us
  transfers between devices with their start and end apart: 4, of which 4 were waited for; matrix products, arithmetic and copies ran while one was open for 0% of the time, Pallas kernels for 0%

profile of v1, /device:TPU:16, one launch (start us, length us, event | category | flops | bytes accessed | tf_op | source)
XLA Modules:
  0.0 164.5 jit_solution(377106238649781205)
XLA Ops:
  0.0 3.4 %shard_map.82 = (bf16[8,16,1920]{2,1,0:T(8,128)(2,1)S(1)}, f32[4,16,1024]{2,1,0:T(8,128)S(1)}, f32[4,16,128]{2,1,0:T(8,128)S(1)}, f32[2,1024]{1,0:T(2,128)S(1)},...) custom-call(s32[4,16]{1,0:T(4,128)} %bitcast.5, s32[16,64]{1,0:T(8,128)} %bitcast.4, ...), custom_call_target="tpu_custom_call" | custom-call | tf_op jit(solution)/shard_map/pallas_call | solution.py:138
  3.4 25.1 %all_to_all.40.got_ref = bf16[8,16,1920]{2,1,0:T(8,128)(2,1)S(1)} all-to-all(bf16[8,16,1920]{2,1,0:T(8,128)(2,1)S(1)} %get-tuple-element.14), channel_id=1, replica_groups=mesh['dp'=2,'section'=16,'tensor'=8] {'tensor'}, dimensions={0} | all-to-all | bytes 983040 | tf_op jit(solution)/shard_map/all_to_all | solution.py:288
  28.4 2.4 %shard_map.83 = (bf16[8,16,512]{2,1,0:T(8,128)(2,1)S(1)}, bf16[2,1024,1024]{2,1,0:T(8,128)(2,1)S(1)}) custom-call(bf16[8,16,1920]{2,1,0:T(8,128)(2,1)S(1)} %all_to_all.40.got_ref, f32[4,16,128]{2,1,0:T(8,128)S(1)} %get-tuple-element.15.table_ref, bf16[1,2,1024,1024]{3,2,1,0:T(8,128)(2,1)} %refs_0_.1), custom_call_target="tpu_custom_call" | custom-call | tf_op jit(solution)/shard_map/pallas_call | solution.py:257
  30.9 11.5 %all_to_all.41.got_ref = bf16[8,16,512]{2,1,0:T(8,128)(2,1)S(1)} all-to-all(bf16[8,16,512]{2,1,0:T(8,128)(2,1)S(1)} %get-tuple-element.16), channel_id=1, replica_groups=mesh['dp'=2,'section'=16,'tensor'=8] {'tensor'}, dimensions={0} | all-to-all | bytes 262144 | tf_op jit(solution)/shard_map/all_to_all | solution.py:288
  42.3 0.5 shard_map.84
  42.9 7.9 %collective-permute-done.state_ref = f32[4,16,1024]{2,1,0:T(8,128)S(1)} collective-permute-done((f32[4,16,1024]{2,1,0:T(8,128)S(1)}, f32[4,16,1024]{2,1,0:T(8,128)S(1)}, u32[]{:S(2)}, u32[]{:S(2)}) %collective-permute-start) | collective-permute-done | bytes 262176 | tf_op jit(solution)/shard_map/ppermute | solution.py:311
  50.8 0.6 shard_map.85
  51.4 16.7 %all_to_all.42.got_ref = bf16[8,16,1920]{2,1,0:T(8,128)(2,1)S(1)} all-to-all(bf16[8,16,1920]{2,1,0:T(8,128)(2,1)S(1)} %shard_map.85), channel_id=1, replica_groups=mesh['dp'=2,'section'=16,'tensor'=8] {'tensor'}, dimensions={0} | all-to-all | bytes 983040 | tf_op jit(solution)/shard_map/all_to_all | solution.py:288
  68.1 0.6 shard_map.86
  68.6 11.5 %all_to_all.43.got_ref = bf16[8,16,512]{2,1,0:T(8,128)(2,1)S(1)} all-to-all(bf16[8,16,512]{2,1,0:T(8,128)(2,1)S(1)} %shard_map.86), channel_id=1, replica_groups=mesh['dp'=2,'section'=16,'tensor'=8] {'tensor'}, dimensions={0} | all-to-all | bytes 262144 | tf_op jit(solution)/shard_map/all_to_all | solution.py:288
  80.1 0.5 shard_map.87
  80.7 7.9 %collective-permute-done.1.state_ref = f32[4,16,1024]{2,1,0:T(8,128)S(1)} collective-permute-done((f32[4,16,1024]{2,1,0:T(8,128)S(1)}, f32[4,16,1024]{2,1,0:T(8,128)S(1)}, u32[]{:S(2)}, u32[]{:S(2)}) %collective-permute-start.1) | collective-permute-done | bytes 262176 | tf_op jit(solution)/shard_map/ppermute | solution.py:311
  88.6 0.6 shard_map.88
  89.2 16.7 %all_to_all.44.got_ref = bf16[8,16,1920]{2,1,0:T(8,128)(2,1)S(1)} all-to-all(bf16[8,16,1920]{2,1,0:T(8,128)(2,1)S(1)} %shard_map.88), channel_id=1, replica_groups=mesh['dp'=2,'section'=16,'tensor'=8] {'tensor'}, dimensions={0} | all-to-all | bytes 983040 | tf_op jit(solution)/shard_map/all_to_all | solution.py:288
  105.8 0.6 shard_map.89
  106.4 11.5 %all_to_all.45.got_ref = bf16[8,16,512]{2,1,0:T(8,128)(2,1)S(1)} all-to-all(bf16[8,16,512]{2,1,0:T(8,128)(2,1)S(1)} %shard_map.89), channel_id=1, replica_groups=mesh['dp'=2,'section'=16,'tensor'=8] {'tensor'}, dimensions={0} | all-to-all | bytes 262144 | tf_op jit(solution)/shard_map/all_to_all | solution.py:288
  117.8 0.5 shard_map.90
  118.4 7.9 %collective-permute-done.2.state_ref = f32[4,16,1024]{2,1,0:T(8,128)S(1)} collective-permute-done((f32[4,16,1024]{2,1,0:T(8,128)S(1)}, f32[4,16,1024]{2,1,0:T(8,128)S(1)}, u32[]{:S(2)}, u32[]{:S(2)}) %collective-permute-start.2) | collective-permute-done | bytes 262176 | tf_op jit(solution)/shard_map/ppermute | solution.py:311
  126.3 0.6 shard_map.91
  126.9 16.4 %all_to_all.46.got_ref = bf16[8,16,1920]{2,1,0:T(8,128)(2,1)S(1)} all-to-all(bf16[8,16,1920]{2,1,0:T(8,128)(2,1)S(1)} %shard_map.91), channel_id=1, replica_groups=mesh['dp'=2,'section'=16,'tensor'=8] {'tensor'}, dimensions={0} | all-to-all | bytes 983040 | tf_op jit(solution)/shard_map/all_to_all | solution.py:288
  143.3 0.6 shard_map.92
  143.8 11.5 %all_to_all.47.got_ref = bf16[8,16,512]{2,1,0:T(8,128)(2,1)S(1)} all-to-all(bf16[8,16,512]{2,1,0:T(8,128)(2,1)S(1)} %shard_map.92), channel_id=1, replica_groups=mesh['dp'=2,'section'=16,'tensor'=8] {'tensor'}, dimensions={0} | all-to-all | bytes 262144 | tf_op jit(solution)/shard_map/all_to_all | solution.py:288
  155.9 7.9 %collective-permute-done.3 = f32[4,16,1024]{2,1,0:T(8,128)S(1)} collective-permute-done((f32[4,16,1024]{2,1,0:T(8,128)S(1)}, f32[4,16,1024]{2,1,0:T(8,128)S(1)}, u32[]{:S(2)}, u32[]{:S(2)}) %collective-permute-start.3) | collective-permute-done | bytes 262176 | tf_op jit(solution)/shard_map/ppermute | solution.py:311
  163.8 0.7 copy.10
  (5 shorter events, 0.8 us)
Async XLA Ops:
  42.8 8.0 %collective-permute-start = (f32[4,16,1024]{2,1,0:T(8,128)S(1)}, f32[4,16,1024]{2,1,0:T(8,128)S(1)}, u32[]{:S(2)}, u32[]{:S(2)}) collective-permute-start(f32[4,16,1024]{2,1,0:T(8,128)S(1)} %shard_map.84), channel_id=1, source_target_pairs={{0,8},{8,16},{16,24},{24,32},{32,40},{40,48},{48,56},{56,64},{64,7... | collective-permute-start | bytes 786440 | tf_op jit(solution)/shard_map/ppermute | solution.py:311
  80.6 8.0 %collective-permute-start.1 = (f32[4,16,1024]{2,1,0:T(8,128)S(1)}, f32[4,16,1024]{2,1,0:T(8,128)S(1)}, u32[]{:S(2)}, u32[]{:S(2)}) collective-permute-start(f32[4,16,1024]{2,1,0:T(8,128)S(1)} %shard_map.87), channel_id=1, source_target_pairs={{0,8},{8,16},{16,24},{24,32},{32,40},{40,48},{48,56},{56,64},{64,7... | collective-permute-start | bytes 786440 | tf_op jit(solution)/shard_map/ppermute | solution.py:311
  118.3 8.0 %collective-permute-start.2 = (f32[4,16,1024]{2,1,0:T(8,128)S(1)}, f32[4,16,1024]{2,1,0:T(8,128)S(1)}, u32[]{:S(2)}, u32[]{:S(2)}) collective-permute-start(f32[4,16,1024]{2,1,0:T(8,128)S(1)} %shard_map.90), channel_id=1, source_target_pairs={{0,8},{8,16},{16,24},{24,32},{32,40},{40,48},{48,56},{56,64},{64,7... | collective-permute-start | bytes 786440 | tf_op jit(solution)/shard_map/ppermute | solution.py:311
  155.8 8.0 %collective-permute-start.3 = (f32[4,16,1024]{2,1,0:T(8,128)S(1)}, f32[4,16,1024]{2,1,0:T(8,128)S(1)}, u32[]{:S(2)}, u32[]{:S(2)}) collective-permute-start(f32[4,16,1024]{2,1,0:T(8,128)S(1)} %shard_map.93), channel_id=1, source_target_pairs={{0,8},{8,16},{16,24},{24,32},{32,40},{40,48},{48,56},{56,64},{64,7... | collective-permute-start | bytes 786440 | tf_op jit(solution)/shard_map/ppermute | solution.py:311

commit v2 on v1

--- a/solution.py
+++ b/solution.py
@@ -22,6 +22,7 @@
 MIX = 768
 PIECE = 896
 CHUNKS = 8
+TOP = 125.0
 VMEM_LIMIT = 16 * 1024 * 1024
 
 VMEM = pl.BlockSpec(memory_space=pltpu.VMEM)
@@ -61,13 +62,28 @@
             out_ref[2 * slot + half, :, MIX:PIECE] = pair[here]
 
 
-def write_cache(out_ref, cache_ref, step):
+def chunks_of(cache_ref):
+    return range(cache_ref.shape[2] // TREE)
+
+
+def write_cache(out_ref, cache_ref, step, start):
     for slot in range(cache_ref.shape[1]):
-        for chunk in range(cache_ref.shape[2] // TREE):
+        for chunk in chunks_of(cache_ref):
             block = cache_ref[step, slot, chunk * TREE : (chunk + 1) * TREE, :]
-            start = PIECE + chunk * BOTH
+            place = start + chunk * BOTH
             for half in range(2):
-                out_ref[2 * slot + half, :, start : start + BOTH] = block
+                out_ref[2 * slot + half, :, place : place + BOTH] = block
+
+
+def write_sides(out_ref, cache_ref, step, start):
+    for slot in range(cache_ref.shape[1]):
+        for chunk in chunks_of(cache_ref):
+            here = slice(chunk * TREE, (chunk + 1) * TREE)
+            place = start + chunk * HEAD
+            for half in range(2):
+                out_ref[2 * slot + half, :, place : place + HEAD] = cache_ref[
+                    step, slot, here, half * HEAD : (half + 1) * HEAD
+                ]
 
 
 def first_kernel(
@@ -75,11 +91,7 @@
     out_ref, state_ref, table_ref, gain_ref, weight_ref, cache_ref,
     assign_ref, parents_ref, lengths_ref, rows, sems, more,
 ):
-    layers = weight_ref.shape[0]
-    weight_copies = [
-        loads(weight_far.at[0, layer], weight_ref.at[layer], sems.at[layer])
-        for layer in range(layers)
-    ]
+    weight_copies = loads(weight_far.at[0, 0], weight_ref, sems)
     other = [
         pltpu.make_async_copy(source, target, more.at[index])
         for index, (source, target) in enumerate(
@@ -87,13 +99,13 @@
                 (assign_far, assign_ref),
                 (parents_far, parents_ref),
                 (lengths_far, lengths_ref),
-                (state_far.at[0], state_ref),
+                (state_far, state_ref),
                 (gain_far.at[0], gain_ref),
                 (cache_far.at[0], cache_ref),
             )
         )
     ]
-    for copy in other[:5] + weight_copies[0] + other[5:] + sum(weight_copies[1:], []):
+    for copy in other[:5] + weight_copies + other[5:]:
         copy.start()
     for copy in other[:3]:
         copy.wait()
@@ -116,33 +128,32 @@
         table_ref[step] = jnp.where(lane < TREE, rows[step], live)
     other[3].wait()
     other[4].wait()
-    slots, tree, width = state_ref.shape
-    state = state_ref[...].reshape(slots * tree, width)
+    width = state_ref.shape[1]
+    state = state_ref[...]
     scaled = (state * gain_ref[0:1, :]).astype(bf16)
-    depth = width // len(weight_copies[0])
-    raw = jnp.zeros((slots * tree, weight_ref.shape[2]), f32)
-    for part, copy in enumerate(weight_copies[0]):
+    depth = width // len(weight_copies)
+    raw = jnp.zeros((state.shape[0], weight_ref.shape[1]), f32)
+    for part, copy in enumerate(weight_copies):
         copy.wait()
         span = slice(part * depth, (part + 1) * depth)
-        raw = raw + jnp.dot(scaled[:, span], weight_ref[0, span, :], preferred_element_type=f32)
+        raw = raw + jnp.dot(scaled[:, span], weight_ref[span, :], preferred_element_type=f32)
     write_pieces(out_ref, raw, state)
     other[5].wait()
-    write_cache(out_ref, cache_ref, 0)
-    for copy in sum(weight_copies[1:], []):
-        copy.wait()
+    write_cache(out_ref, cache_ref, 0, PIECE)
 
 
 def first(assign, parents, lengths, hidden, gain, weight, cache):
     _, slots, tree, width = hidden.shape
     steps, _, span = cache.shape[1:4]
+    rows = hidden.reshape(slots * tree, width)
     return pl.pallas_call(
         first_kernel,
         out_shape=(
             jax.ShapeDtypeStruct((2 * slots, TREE, PIECE + span // TREE * BOTH), bf16),
-            pltpu.VMEM((slots, tree, width), f32),
+            pltpu.VMEM((slots * tree, width), f32),
             pltpu.VMEM((steps, TREE, HEAD), f32),
             pltpu.VMEM(gain.shape[1:], f32),
-            pltpu.VMEM(weight.shape[1:], bf16),
+            pltpu.VMEM(weight.shape[2:], bf16),
             pltpu.VMEM(cache.shape[1:], bf16),
         ),
         in_specs=[FAR] * 7,
@@ -152,47 +163,114 @@
             pltpu.SMEM(parents.shape[::-1], jnp.int32),
             pltpu.SMEM(lengths.shape, jnp.int32),
             pltpu.VMEM((steps, TREE, HEAD), f32),
-            pltpu.SemaphoreType.DMA((weight.shape[1], CHUNKS)),
+            pltpu.SemaphoreType.DMA((CHUNKS,)),
             pltpu.SemaphoreType.DMA((6,)),
         ],
         compiler_params=PARAMS,
-    )(*(far(value) for value in (assign.T, parents.T, lengths, hidden, gain, weight, cache)))
-
-
-def project_kernel(state_ref, gain_ref, weight_ref, cache_ref, out_ref, *, step):
-    slots, tree, width = state_ref.shape
-    state = state_ref[...].reshape(slots * tree, width)
+    )(*map(far, (assign.T, parents.T, lengths, rows, gain, weight, cache)))
+
+
+def rest_kernel(in_far, out_far, _, in_ref, out_ref, sems):
+    copies = loads(in_far.at[0, 1], in_ref, sems.at[0]) + loads(out_far.at[0, 1], out_ref, sems.at[1])
+    for copy in copies:
+        copy.start()
+    for copy in copies:
+        copy.wait()
+
+
+def rest(weight_in, weight_out, after):
+    return pl.pallas_call(
+        rest_kernel,
+        out_shape=tuple(pltpu.VMEM(w.shape[2:], bf16) for w in (weight_in, weight_out)),
+        in_specs=[FAR] * 2 + [VMEM],
+        out_specs=(VMEM,) * 2,
+        scratch_shapes=[pltpu.SemaphoreType.DMA((2, CHUNKS))],
+        compiler_params=PARAMS,
+    )(far(weight_in), far(weight_out), after)
+
+
+def pick(step, act, layers):
+    if len(layers) == 1:
+        return act(layers[0])
     which = layer_of(step)
-    scaled = (state * gain_ref[pl.ds(which, 1), :]).astype(bf16)
-    raw = jnp.dot(scaled, weight_ref[which], preferred_element_type=f32)
-    write_pieces(out_ref, raw, state)
-    write_cache(out_ref, cache_ref, step)
-
-
-def project(state, gain, weight, cache, step):
-    slots, span = cache.shape[1:3]
+    for index, layer in enumerate(layers):
+        pl.when(which == index)(functools.partial(act, layer))
+
+
+def unit_of(power):
+    return jnp.exp2(power) / jnp.where(power < TOP, 32767.0, 4095.0)
+
+
+def pack(packed_ref, state):
+    width = state.shape[1]
+    peak = jnp.max(jnp.abs(state), axis=-1, keepdims=True)
+    power = jnp.clip(jnp.ceil(jnp.log2(jnp.maximum(peak, 1e-37))), -TOP, TOP)
+    ratio = state * jnp.exp2(-power) * jnp.where(power < TOP, 32767.0, 4095.0)
+    steps = jnp.clip(jnp.round(ratio), -32767.0, 32767.0)
+    packed_ref[:, :width] = steps.astype(jnp.int32).astype(jnp.int16)
+    powers = jnp.broadcast_to(power.astype(jnp.int32), (state.shape[0], HEAD))
+    packed_ref[:, width:] = powers.astype(jnp.int16)
+
+
+def unpack(packed_ref):
+    width = packed_ref.shape[1] - HEAD
+    power = packed_ref[:, width:].astype(jnp.int32).astype(f32)[:, :1]
+    return packed_ref[:, :width].astype(jnp.int32).astype(f32) * unit_of(power)
+
+
+def expand_kernel(packed_ref, out_ref):
+    out_ref[...] = unpack(packed_ref)
+
+
+def expand(packed):
+    rows, width = packed.shape
+    return pl.pallas_call(
+        expand_kernel,
+        out_shape=jax.ShapeDtypeStruct((rows, width - HEAD), f32),
+        in_specs=[VMEM],
+        out_specs=VMEM,
+        compiler_params=PARAMS,
+    )(packed)
+
+
+def project_kernel(packed_ref, mine_ref, come_ref, gain_ref, *refs, step):
+    *weight_refs, out_ref, state_ref, sides_ref = refs
+    side = lax.rem(lax.axis_index("tensor"), 2)
+    sides_ref[side] = mine_ref[...]
+    sides_ref[1 - side] = come_ref[...]
+    state = unpack(packed_ref)
+    state_ref[...] = state
+    scaled = (state * gain_ref[pl.ds(layer_of(step), 1), :]).astype(bf16)
+
+    def act(weight_ref):
+        raw = jnp.dot(scaled, weight_ref[...], preferred_element_type=f32)
+        write_pieces(out_ref, raw, state)
+
+    pick(step, act, weight_refs)
+
+
+def project(packed, mine, come, gain, weights, step):
+    rows, width = packed.shape
     return pl.pallas_call(
         functools.partial(project_kernel, step=step),
-        out_shape=jax.ShapeDtypeStruct((2 * slots, TREE, PIECE + span // TREE * BOTH), bf16),
-        in_specs=[VMEM] * 4,
-        out_specs=VMEM,
-        compiler_params=PARAMS,
-    )(state, gain, weight, cache)
-
-
-def attend_kernel(got_ref, table_ref, *refs, step):
+        out_shape=(
+            jax.ShapeDtypeStruct((mine.shape[0], TREE, PIECE), bf16),
+            jax.ShapeDtypeStruct((rows, width - HEAD), f32),
+            jax.ShapeDtypeStruct((2,) + mine.shape, bf16),
+        ),
+        in_specs=[VMEM] * (4 + len(weights)),
+        out_specs=(VMEM,) * 3,
+        compiler_params=PARAMS,
+    )(packed, mine, come, gain, *weights)
+
+
+def attend_kernel(got_ref, table_ref, cache_ref, *refs, step):
     if step:
-        (out_ref,) = refs
+        sides_ref, out_ref = refs
         copies = []
     else:
         weight_far, out_ref, weight_ref, sems = refs
-        copies = sum(
-            (
-                loads(weight_far.at[0, layer], weight_ref.at[layer], sems.at[layer])
-                for layer in range(weight_ref.shape[0])
-            ),
-            [],
-        )
+        copies = loads(weight_far.at[0, 0], weight_ref, sems)
     for copy in copies:
         copy.start()
     total = jnp.sum(got_ref[:, :, :PIECE].astype(f32), axis=0)
@@ -205,17 +283,25 @@
     )
     tree_keys = projected[:, HALF : HALF + HEAD]
     tree_values = projected[:, HALF + HEAD :]
-    keys, values = (
-        jnp.concatenate(
+    if step:
+        blocks = [
             [
-                got_ref[piece, :, start + side : start + side + HEAD]
+                sides_ref[side, piece, :, start : start + HEAD]
+                for piece in range(sides_ref.shape[1])
+                for start in range(0, sides_ref.shape[3], HEAD)
+            ]
+            for side in range(2)
+        ]
+    else:
+        blocks = [
+            [
+                got_ref[piece, :, start + side * HEAD : start + (side + 1) * HEAD]
                 for piece in range(got_ref.shape[0])
                 for start in range(PIECE, got_ref.shape[2], BOTH)
-            ],
-            axis=0,
-        )
-        for side in (0, HEAD)
-    )
+            ]
+            for side in range(2)
+        ]
+    keys, values = (jnp.concatenate(block, axis=0) for block in blocks)
     contract = (((1,), (1,)), ((), ()))
     scaling = HEAD ** (-0.5)
     scores = lax.dot_general(queries, keys, contract, preferred_element_type=f32)
@@ -243,45 +329,68 @@
         part = attended[h * TREE : (h + 1) * TREE]
         for piece in range(out_ref.shape[0]):
             out_ref[piece, :, h * HEAD : (h + 1) * HEAD] = part
+    if step + 1 < cache_ref.shape[0]:
+        write_sides(out_ref, cache_ref, step + 1, HALF)
     for copy in copies:
         copy.wait()
 
 
-def attend(got, table, step, weight=None):
-    out_shape = (jax.ShapeDtypeStruct((got.shape[0], TREE, HALF), bf16),)
-    extra, scratch = (), []
+def attend(got, table, cache, step, sides=None, weight=None):
+    steps, _, span = cache.shape[:3]
+    width = HALF + (span // TREE * HEAD if step + 1 < steps else 0)
+    out_shape = (jax.ShapeDtypeStruct((got.shape[0], TREE, width), bf16),)
+    extra, scratch = (sides,), []
+    specs = [VMEM] * 4
     if weight is not None:
-        out_shape += (pltpu.VMEM(weight.shape[1:], bf16),)
+        out_shape += (pltpu.VMEM(weight.shape[2:], bf16),)
         extra = (far(weight),)
-        scratch = [pltpu.SemaphoreType.DMA((weight.shape[1], CHUNKS))]
+        specs[3] = FAR
+        scratch = [pltpu.SemaphoreType.DMA((CHUNKS,))]
     return pl.pallas_call(
         functools.partial(attend_kernel, step=step),
         out_shape=out_shape,
-        in_specs=[VMEM] * 2 + [FAR] * len(extra),
+        in_specs=specs,
         out_specs=(VMEM,) * len(out_shape),
         scratch_shapes=scratch,
         compiler_params=PARAMS,
-    )(got, table, *extra)
-
-
-def update_kernel(state_ref, got_ref, weight_ref, out_ref, *, step):
-    slots = got_ref.shape[0] // 2
+    )(got, table, cache, *extra)
+
+
+def update_kernel(state_ref, got_ref, *refs, step, last):
+    if last:
+        *weight_refs, out_ref = refs
+    else:
+        *weight_refs, out_ref, side_ref = refs
+        side_ref[...] = got_ref[:, :, HALF:]
     attended = jnp.concatenate(
-        [jnp.concatenate([got_ref[2 * s], got_ref[2 * s + 1]], axis=1) for s in range(slots)],
+        [
+            jnp.concatenate([got_ref[at, :, :HALF], got_ref[at + 1, :, :HALF]], axis=1)
+            for at in range(0, got_ref.shape[0], 2)
+        ],
         axis=0,
     )
-    delta = jnp.dot(attended, weight_ref[layer_of(step)], preferred_element_type=f32)
-    out_ref[...] = state_ref[...] + delta.reshape(out_ref.shape)
-
-
-def update(state, got, weight, step):
-    return pl.pallas_call(
-        functools.partial(update_kernel, step=step),
-        out_shape=jax.ShapeDtypeStruct(state.shape, f32),
-        in_specs=[VMEM] * 3,
-        out_specs=VMEM,
-        compiler_params=PARAMS,
-    )(state, got, weight)
+
+    def act(weight_ref):
+        delta = jnp.dot(attended, weight_ref[...], preferred_element_type=f32)
+        pack(out_ref, state_ref[...] + delta)
+
+    pick(step, act, weight_refs)
+
+
+def update(state, got, weights, step):
+    rows, width = state.shape
+    count, tree, total = got.shape
+    out_shape = (jax.ShapeDtypeStruct((rows, width + HEAD), jnp.int16),)
+    last = total == HALF
+    if not last:
+        out_shape += (jax.ShapeDtypeStruct((count, tree, total - HALF), bf16),)
+    return pl.pallas_call(
+        functools.partial(update_kernel, step=step, last=last),
+        out_shape=out_shape,
+        in_specs=[VMEM] * (2 + len(weights)),
+        out_specs=(VMEM,) * len(out_shape),
+        compiler_params=PARAMS,
+    )(state, got, *weights)
 
 
 def exchange(value):
@@ -298,18 +407,25 @@
     pieces, state, table, gain, weight_in, cache = first(
         assign, parents, lengths, hidden_in, norm_gain, w_qkv, kv_cache
     )
-    weight_out = None
+    weights_in = (weight_in,)
+    mates = [(t, t ^ 1) for t in range(pieces.shape[0])]
     for step in range(kv_cache.shape[1]):
         if step:
-            pieces = project(state, gain, weight_in, cache, step)
-        got = exchange(pieces)
-        if step:
-            (spread,) = attend(got, table, step)
+            pieces, state, sides = project(packed, mine, come, gain, weights_in, step)
+            (spread,) = attend(exchange(pieces), table, cache, step, sides)
         else:
-            spread, weight_out = attend(got, table, step, w_out)
-        state = update(state, exchange(spread), weight_out, step)
-        state = lax.ppermute(state, "section", ring)
-    return state[None]
+            spread, weight_out = attend(exchange(pieces), table, cache, step, weight=w_out)
+            weights_out = (weight_out,)
+        packed, *mine = update(state, exchange(spread), weights_out, step)
+        if not step:
+            more_in, more_out = rest(w_qkv, w_out, packed)
+            weights_in += (more_in,)
+            weights_out += (more_out,)
+        packed = lax.ppermute(packed, "section", ring)
+        if mine:
+            (mine,) = mine
+            come = lax.ppermute(mine, "tensor", mates)
+    return expand(packed).reshape(hidden_in.shape)
 
 
 def solution(mesh):

time: 165 us -> 158 us (0.958)
  waiting for transfers between devices: 31.6 us -> 22.3 us
  Pallas kernels: 11.2 us -> 13.6 us
  blocking collectives: 121 us -> 119 us
  starting transfers between devices: 0.33 us -> 2.3 us
    ppermute x4 -> x7, waiting for transfers between devices: 31.6 us -> 22.3 us  [the longest x3 11.8 us: body(): come = lax.ppermute(mine, 'tensor', mates)]
    pallas_call x7 -> x9, Pallas kernels: 3.68 us -> 7.78 us  [the longest x4 2.49 us: update(): pl.pallas_call(functools.partial(update_kernel, step=step, last=last), ou...]
    ppermute x4 -> x7, starting transfers between devices: 0.33 us -> 2.3 us  [the longest x3 1.96 us: body(): come = lax.ppermute(mine, 'tensor', mates)]
  transfers between devices with their start and end apart: 4 -> 7, of which waited for: 4 -> 7; matrix products, arithmetic and copies ran while one was open for 0% -> 0% of each run, Pallas kernels for 0% -> 2%
where the time goes in v2:
time: 158 us
  blocking collectives  119 us (75%)
  waiting for transfers between devices  22.3 us (14%)
  Pallas kernels  13.6 us (9%)
  starting transfers between devices  2.3 us (1%)
    all_to_all x8, blocking collectives, exchange(): return lax.all_to_all(value, 'tensor', 0, 0, tiled=True)  119 us
    ppermute x3, waiting for transfers between devices, body(): come = lax.ppermute(mine, 'tensor', mates)  11.8 us
    ppermute x4, waiting for transfers between devices, body(): packed = lax.ppermute(packed, 'section', ring)  10.4 us
    pallas_call x4, Pallas kernels, attend(): pl.pallas_call(functools.partial(attend_kernel, step=step), out_shape=out...  3.33 us
  transfers between devices with their start and end apart: 7, of which 7 were waited for; matrix products, arithmetic and copies ran while one was open for 0% of the time, Pallas kernels for 2%

profile of v2, /device:TPU:16, one launch (start us, length us, event | category | flops | bytes accessed | tf_op | source)
XLA Modules:
  0.0 157.7 jit_solution(12571979347667252208)
XLA Ops:
  0.0 2.5 %shard_map.82 = (bf16[8,16,1920]{2,1,0:T(8,128)(2,1)S(1)}, f32[64,1024]{1,0:T(8,128)S(1)}, f32[4,16,128]{2,1,0:T(8,128)S(1)}, f32[2,1024]{1,0:T(2,128)S(1)}, bf1...) custom-call(s32[4,16]{1,0:T(4,128)} %bitcast.6, s32[16,64]{1,0:T(8,128)} %bitcast.5, s32[64]{0:T(128)} %lengths_far.1, ...), custom_call_target="tpu_custom_call" | custom-call | tf_op jit(solution)/shard_map/pallas_call | solution.py:149
  2.5 25.1 %all_to_all.40.got_ref = bf16[8,16,1920]{2,1,0:T(8,128)(2,1)S(1)} all-to-all(bf16[8,16,1920]{2,1,0:T(8,128)(2,1)S(1)} %get-tuple-element.31), channel_id=1, replica_groups=mesh['dp'=2,'section'=16,'tensor'=8] {'tensor'}, dimensions={0} | all-to-all | bytes 983040 | tf_op jit(solution)/shard_map/all_to_all | solution.py:397
  27.5 1.6 %shard_map.83 = (bf16[8,16,1024]{2,1,0:T(8,128)(2,1)S(1)}, bf16[1024,1024]{1,0:T(8,128)(2,1)S(1)}) custom-call(bf16[8,16,1920]{2,1,0:T(8,128)(2,1)S(1)} %all_to_all.40.got_ref, f32[4,16,128]{2,1,0:T(8,128)S(1)} %get-tuple-element.32.table_ref, bf16[4,4,64,256]{3,2,1,0:T(8,128)(2,1)S(1)} %get-tuple-element.33.cache_ref, bf16[1,2,1024,1024]{3,2,1,0:T(8,128)(2,1)} %out_far.1), custom_call_target="tpu_custom_call" | custom-call | tf_op jit(solution)/shard_map/pallas_call | solution.py:349
  29.2 12.9 %all_to_all.41.got_ref = bf16[8,16,1024]{2,1,0:T(8,128)(2,1)S(1)} all-to-all(bf16[8,16,1024]{2,1,0:T(8,128)(2,1)S(1)} %get-tuple-element.34), channel_id=1, replica_groups=mesh['dp'=2,'section'=16,'tensor'=8] {'tensor'}, dimensions={0} | all-to-all | bytes 524288 | tf_op jit(solution)/shard_map/all_to_all | solution.py:397
  43.4 2.4 %shard_map.85 = (bf16[1024,1280]{1,0:T(8,128)(2,1)S(1)}, bf16[1024,1024]{1,0:T(8,128)(2,1)S(1)}) custom-call(bf16[1,2,1024,1280]{3,2,1,0:T(8,128)(2,1)} %in_far.1, bf16[1,2,1024,1024]{3,2,1,0:T(8,128)(2,1)} %out_far.1, s16[64,1152]{1,0:T(8,128)(2,1)S(1)} %get-tuple-element.36._), custom_call_target="tpu_custom_call" | custom-call | tf_op jit(solution)/shard_map/pallas_call | solution.py:182
  45.9 2.9 %collective-permute-done.1.come_ref = bf16[8,16,512]{2,1,0:T(8,128)(2,1)S(1)} collective-permute-done((bf16[8,16,512]{2,1,0:T(8,128)(2,1)S(1)}, bf16[8,16,512]{2,1,0:T(8,128)(2,1)S(1)}, u32[]{:S(2)}, u32[]{:S(2)}) %collective-permute-start.1) | collective-permute-done | bytes 131104 | tf_op jit(solution)/shard_map/ppermute | solution.py:427
  48.8 0.7 collective-permute-done.packed_ref
  49.5 0.7 shard_map.86
  50.2 13.9 %all_to_all.42.got_ref = bf16[8,16,896]{2,1,0:T(8,128)(2,1)S(1)} all-to-all(bf16[8,16,896]{2,1,0:T(8,128)(2,1)S(1)} %get-tuple-element.42), channel_id=1, replica_groups=mesh['dp'=2,'section'=16,'tensor'=8] {'tensor'}, dimensions={0} | all-to-all | bytes 458752 | tf_op jit(solution)/shard_map/all_to_all | solution.py:397
  64.7 13.4 %all_to_all.43.got_ref = bf16[8,16,1024]{2,1,0:T(8,128)(2,1)S(1)} all-to-all(bf16[8,16,1024]{2,1,0:T(8,128)(2,1)S(1)} %shard_map.87), channel_id=1, replica_groups=mesh['dp'=2,'section'=16,'tensor'=8] {'tensor'}, dimensions={0} | all-to-all | bytes 524288 | tf_op jit(solution)/shard_map/all_to_all | solution.py:397
  78.8 0.7 collective-permute-start.3
  79.4 4.4 %collective-permute-done.3.come_ref = bf16[8,16,512]{2,1,0:T(8,128)(2,1)S(1)} collective-permute-done((bf16[8,16,512]{2,1,0:T(8,128)(2,1)S(1)}, bf16[8,16,512]{2,1,0:T(8,128)(2,1)S(1)}, u32[]{:S(2)}, u32[]{:S(2)}) %collective-permute-start.3) | collective-permute-done | bytes 131104 | tf_op jit(solution)/shard_map/ppermute | solution.py:427
  83.8 1.6 %collective-permute-done.2.packed_ref = s16[64,1152]{1,0:T(8,128)(2,1)S(1)} collective-permute-done((s16[64,1152]{1,0:T(8,128)(2,1)S(1)}, s16[64,1152]{1,0:T(8,128)(2,1)S(1)}, u32[]{:S(2)}, u32[]{:S(2)}) %collective-permute-start.2) | collective-permute-done | bytes 147488 | tf_op jit(solution)/shard_map/ppermute | solution.py:424
  85.4 0.7 shard_map.89
  86.1 14.1 %all_to_all.44.got_ref = bf16[8,16,896]{2,1,0:T(8,128)(2,1)S(1)} all-to-all(bf16[8,16,896]{2,1,0:T(8,128)(2,1)S(1)} %get-tuple-element.48), channel_id=1, replica_groups=mesh['dp'=2,'section'=16,'tensor'=8] {'tensor'}, dimensions={0} | all-to-all | bytes 458752 | tf_op jit(solution)/shard_map/all_to_all | solution.py:397
  100.8 14.7 %all_to_all.45.got_ref = bf16[8,16,1024]{2,1,0:T(8,128)(2,1)S(1)} all-to-all(bf16[8,16,1024]{2,1,0:T(8,128)(2,1)S(1)} %shard_map.90), channel_id=1, replica_groups=mesh['dp'=2,'section'=16,'tensor'=8] {'tensor'}, dimensions={0} | all-to-all | bytes 524288 | tf_op jit(solution)/shard_map/all_to_all | solution.py:397
  116.2 0.7 collective-permute-start.5
  116.9 4.6 %collective-permute-done.5.come_ref = bf16[8,16,512]{2,1,0:T(8,128)(2,1)S(1)} collective-permute-done((bf16[8,16,512]{2,1,0:T(8,128)(2,1)S(1)}, bf16[8,16,512]{2,1,0:T(8,128)(2,1)S(1)}, u32[]{:S(2)}, u32[]{:S(2)}) %collective-permute-start.5) | collective-permute-done | bytes 131104 | tf_op jit(solution)/shard_map/ppermute | solution.py:427
  121.4 1.5 collective-permute-done.4.packed_ref
  122.9 0.7 shard_map.92
  123.6 13.9 %all_to_all.46.got_ref = bf16[8,16,896]{2,1,0:T(8,128)(2,1)S(1)} all-to-all(bf16[8,16,896]{2,1,0:T(8,128)(2,1)S(1)} %get-tuple-element.53), channel_id=1, replica_groups=mesh['dp'=2,'section'=16,'tensor'=8] {'tensor'}, dimensions={0} | all-to-all | bytes 458752 | tf_op jit(solution)/shard_map/all_to_all | solution.py:397
  138.1 11.5 %all_to_all.47.got_ref = bf16[8,16,512]{2,1,0:T(8,128)(2,1)S(1)} all-to-all(bf16[8,16,512]{2,1,0:T(8,128)(2,1)S(1)} %shard_map.93), channel_id=1, replica_groups=mesh['dp'=2,'section'=16,'tensor'=8] {'tensor'}, dimensions={0} | all-to-all | bytes 262144 | tf_op jit(solution)/shard_map/all_to_all | solution.py:397
  150.2 6.7 %collective-permute-done.6.packed_ref = s16[64,1152]{1,0:T(8,128)(2,1)S(1)} collective-permute-done((s16[64,1152]{1,0:T(8,128)(2,1)S(1)}, s16[64,1152]{1,0:T(8,128)(2,1)S(1)}, u32[]{:S(2)}, u32[]{:S(2)}) %collective-permute-start.6) | collective-permute-done | bytes 147488 | tf_op jit(solution)/shard_map/ppermute | solution.py:424
  156.9 0.8 shard_map.95
  (12 shorter events, 5.2 us)
Async XLA Ops:
  42.7 6.8 %collective-permute-start = (s16[64,1152]{1,0:T(8,128)(2,1)S(1)}, s16[64,1152]{1,0:T(8,128)(2,1)S(1)}, u32[]{:S(2)}, u32[]{:S(2)}) collective-permute-start(s16[64,1152]{1,0:T(8,128)(2,1)S(1)} %get-tuple-element.36._), channel_id=1, source_target_pairs={{0,8},{8,16},{16,24},{24,32},{32,40},{40,48},{48,56},{56,64},{64,7... | collective-permute-start | bytes 442376 | tf_op jit(solution)/shard_map/ppermute | solution.py:424
  42.8 6.0 %collective-permute-start.1 = (bf16[8,16,512]{2,1,0:T(8,128)(2,1)S(1)}, bf16[8,16,512]{2,1,0:T(8,128)(2,1)S(1)}, u32[]{:S(2)}, u32[]{:S(2)}) collective-permute-start(bf16[8,16,512]{2,1,0:T(8,128)(2,1)S(1)} %get-tuple-element.37.mine_ref), channel_id=1, source_target_pairs={{0,1},{1,0},{2,3},{3,2},{4,5},{5,4},{6,7},{7,6},{8,9},{9,8},{10,11... | collective-permute-start | bytes 393224 | tf_op jit(solution)/shard_map/ppermute | solution.py:427
  78.7 6.8 %collective-permute-start.2 = (s16[64,1152]{1,0:T(8,128)(2,1)S(1)}, s16[64,1152]{1,0:T(8,128)(2,1)S(1)}, u32[]{:S(2)}, u32[]{:S(2)}) collective-permute-start(s16[64,1152]{1,0:T(8,128)(2,1)S(1)} %get-tuple-element.45), channel_id=1, source_target_pairs={{0,8},{8,16},{16,24},{24,32},{32,40},{40,48},{48,56},{56,64},{64,7... | collective-permute-start | bytes 442376 | tf_op jit(solution)/shard_map/ppermute | solution.py:424
  78.8 5.1 %collective-permute-start.3 = (bf16[8,16,512]{2,1,0:T(8,128)(2,1)S(1)}, bf16[8,16,512]{2,1,0:T(8,128)(2,1)S(1)}, u32[]{:S(2)}, u32[]{:S(2)}) collective-permute-start(bf16[8,16,512]{2,1,0:T(8,128)(2,1)S(1)} %get-tuple-element.46.mine_ref), channel_id=1, source_target_pairs={{0,1},{1,0},{2,3},{3,2},{4,5},{5,4},{6,7},{7,6},{8,9},{9,8},{10,11... | collective-permute-start | bytes 393224 | tf_op jit(solution)/shard_map/ppermute | solution.py:427
  116.1 6.8 %collective-permute-start.4 = (s16[64,1152]{1,0:T(8,128)(2,1)S(1)}, s16[64,1152]{1,0:T(8,128)(2,1)S(1)}, u32[]{:S(2)}, u32[]{:S(2)}) collective-permute-start(s16[64,1152]{1,0:T(8,128)(2,1)S(1)} %get-tuple-element.50), channel_id=1, source_target_pairs={{0,8},{8,16},{16,24},{24,32},{32,40},{40,48},{48,56},{56,64},{64,7... | collective-permute-start | bytes 442376 | tf_op jit(solution)/shard_map/ppermute | solution.py:424
  116.2 5.2 %collective-permute-start.5 = (bf16[8,16,512]{2,1,0:T(8,128)(2,1)S(1)}, bf16[8,16,512]{2,1,0:T(8,128)(2,1)S(1)}, u32[]{:S(2)}, u32[]{:S(2)}) collective-permute-start(bf16[8,16,512]{2,1,0:T(8,128)(2,1)S(1)} %get-tuple-element.51.mine_ref), channel_id=1, source_target_pairs={{0,1},{1,0},{2,3},{3,2},{4,5},{5,4},{6,7},{7,6},{8,9},{9,8},{10,11... | collective-permute-start | bytes 393224 | tf_op jit(solution)/shard_map/ppermute | solution.py:427
  150.2 6.8 %collective-permute-start.6 = (s16[64,1152]{1,0:T(8,128)(2,1)S(1)}, s16[64,1152]{1,0:T(8,128)(2,1)S(1)}, u32[]{:S(2)}, u32[]{:S(2)}) collective-permute-start(s16[64,1152]{1,0:T(8,128)(2,1)S(1)} %shard_map.94), channel_id=1, source_target_pairs={{0,8},{8,16},{16,24},{24,32},{32,40},{40,48},{48,56},{56,64},{64,7... | collective-permute-start | bytes 442376 | tf_op jit(solution)/shard_map/ppermute | solution.py:424

commit v3 on v2

--- a/solution.py
+++ b/solution.py
@@ -22,7 +22,6 @@
 MIX = 768
 PIECE = 896
 CHUNKS = 8
-TOP = 125.0
 VMEM_LIMIT = 16 * 1024 * 1024
 
 VMEM = pl.BlockSpec(memory_space=pltpu.VMEM)
@@ -170,23 +169,23 @@
     )(*map(far, (assign.T, parents.T, lengths, rows, gain, weight, cache)))
 
 
-def rest_kernel(in_far, out_far, _, in_ref, out_ref, sems):
-    copies = loads(in_far.at[0, 1], in_ref, sems.at[0]) + loads(out_far.at[0, 1], out_ref, sems.at[1])
+def rest_kernel(in_far, _, in_ref, sems):
+    copies = loads(in_far.at[0, 1], in_ref, sems)
     for copy in copies:
         copy.start()
     for copy in copies:
         copy.wait()
 
 
-def rest(weight_in, weight_out, after):
+def rest(weight_in, after):
     return pl.pallas_call(
         rest_kernel,
-        out_shape=tuple(pltpu.VMEM(w.shape[2:], bf16) for w in (weight_in, weight_out)),
-        in_specs=[FAR] * 2 + [VMEM],
-        out_specs=(VMEM,) * 2,
-        scratch_shapes=[pltpu.SemaphoreType.DMA((2, CHUNKS))],
-        compiler_params=PARAMS,
-    )(far(weight_in), far(weight_out), after)
+        out_shape=pltpu.VMEM(weight_in.shape[2:], bf16),
+        in_specs=[FAR, VMEM],
+        out_specs=VMEM,
+        scratch_shapes=[pltpu.SemaphoreType.DMA((CHUNKS,))],
+        compiler_params=PARAMS,
+    )(far(weight_in), after)
 
 
 def pick(step, act, layers):
@@ -197,49 +196,12 @@
         pl.when(which == index)(functools.partial(act, layer))
 
 
-def unit_of(power):
-    return jnp.exp2(power) / jnp.where(power < TOP, 32767.0, 4095.0)
-
-
-def pack(packed_ref, state):
-    width = state.shape[1]
-    peak = jnp.max(jnp.abs(state), axis=-1, keepdims=True)
-    power = jnp.clip(jnp.ceil(jnp.log2(jnp.maximum(peak, 1e-37))), -TOP, TOP)
-    ratio = state * jnp.exp2(-power) * jnp.where(power < TOP, 32767.0, 4095.0)
-    steps = jnp.clip(jnp.round(ratio), -32767.0, 32767.0)
-    packed_ref[:, :width] = steps.astype(jnp.int32).astype(jnp.int16)
-    powers = jnp.broadcast_to(power.astype(jnp.int32), (state.shape[0], HEAD))
-    packed_ref[:, width:] = powers.astype(jnp.int16)
-
-
-def unpack(packed_ref):
-    width = packed_ref.shape[1] - HEAD
-    power = packed_ref[:, width:].astype(jnp.int32).astype(f32)[:, :1]
-    return packed_ref[:, :width].astype(jnp.int32).astype(f32) * unit_of(power)
-
-
-def expand_kernel(packed_ref, out_ref):
-    out_ref[...] = unpack(packed_ref)
-
-
-def expand(packed):
-    rows, width = packed.shape
-    return pl.pallas_call(
-        expand_kernel,
-        out_shape=jax.ShapeDtypeStruct((rows, width - HEAD), f32),
-        in_specs=[VMEM],
-        out_specs=VMEM,
-        compiler_params=PARAMS,
-    )(packed)
-
-
-def project_kernel(packed_ref, mine_ref, come_ref, gain_ref, *refs, step):
-    *weight_refs, out_ref, state_ref, sides_ref = refs
+def project_kernel(state_ref, mine_ref, come_ref, gain_ref, *refs, step):
+    *weight_refs, out_ref, sides_ref = refs
     side = lax.rem(lax.axis_index("tensor"), 2)
     sides_ref[side] = mine_ref[...]
     sides_ref[1 - side] = come_ref[...]
-    state = unpack(packed_ref)
-    state_ref[...] = state
+    state = state_ref[...]
     scaled = (state * gain_ref[pl.ds(layer_of(step), 1), :]).astype(bf16)
 
     def act(weight_ref):
@@ -249,30 +211,21 @@
     pick(step, act, weight_refs)
 
 
-def project(packed, mine, come, gain, weights, step):
-    rows, width = packed.shape
+def project(state, mine, come, gain, weights, step):
     return pl.pallas_call(
         functools.partial(project_kernel, step=step),
         out_shape=(
             jax.ShapeDtypeStruct((mine.shape[0], TREE, PIECE), bf16),
-            jax.ShapeDtypeStruct((rows, width - HEAD), f32),
             jax.ShapeDtypeStruct((2,) + mine.shape, bf16),
         ),
         in_specs=[VMEM] * (4 + len(weights)),
-        out_specs=(VMEM,) * 3,
-        compiler_params=PARAMS,
-    )(packed, mine, come, gain, *weights)
+        out_specs=(VMEM,) * 2,
+        compiler_params=PARAMS,
+    )(state, mine, come, gain, *weights)
 
 
 def attend_kernel(got_ref, table_ref, cache_ref, *refs, step):
-    if step:
-        sides_ref, out_ref = refs
-        copies = []
-    else:
-        weight_far, out_ref, weight_ref, sems = refs
-        copies = loads(weight_far.at[0, 0], weight_ref, sems)
-    for copy in copies:
-        copy.start()
+    *sides_ref, out_ref = refs
     total = jnp.sum(got_ref[:, :, :PIECE].astype(f32), axis=0)
     square = total[:, MIX : MIX + 1] + total[:, MIX + HEAD // 2 : MIX + HEAD // 2 + 1]
     factor = lax.rsqrt(square / D + epsilon)
@@ -286,9 +239,9 @@
     if step:
         blocks = [
             [
-                sides_ref[side, piece, :, start : start + HEAD]
-                for piece in range(sides_ref.shape[1])
-                for start in range(0, sides_ref.shape[3], HEAD)
+                sides_ref[0][side, piece, :, start : start + HEAD]
+                for piece in range(sides_ref[0].shape[1])
+                for start in range(0, sides_ref[0].shape[3], HEAD)
             ]
             for side in range(2)
         ]
@@ -331,36 +284,25 @@
             out_ref[piece, :, h * HEAD : (h + 1) * HEAD] = part
     if step + 1 < cache_ref.shape[0]:
         write_sides(out_ref, cache_ref, step + 1, HALF)
-    for copy in copies:
-        copy.wait()
-
-
-def attend(got, table, cache, step, sides=None, weight=None):
+
+
+def attend(got, table, cache, step, sides=()):
     steps, _, span = cache.shape[:3]
     width = HALF + (span // TREE * HEAD if step + 1 < steps else 0)
-    out_shape = (jax.ShapeDtypeStruct((got.shape[0], TREE, width), bf16),)
-    extra, scratch = (sides,), []
-    specs = [VMEM] * 4
-    if weight is not None:
-        out_shape += (pltpu.VMEM(weight.shape[2:], bf16),)
-        extra = (far(weight),)
-        specs[3] = FAR
-        scratch = [pltpu.SemaphoreType.DMA((CHUNKS,))]
     return pl.pallas_call(
         functools.partial(attend_kernel, step=step),
-        out_shape=out_shape,
-        in_specs=specs,
-        out_specs=(VMEM,) * len(out_shape),
-        scratch_shapes=scratch,
-        compiler_params=PARAMS,
-    )(got, table, cache, *extra)
-
-
-def update_kernel(state_ref, got_ref, *refs, step, last):
+        out_shape=jax.ShapeDtypeStruct((got.shape[0], TREE, width), bf16),
+        in_specs=[VMEM] * (3 + len(sides)),
+        out_specs=VMEM,
+        compiler_params=PARAMS,
+    )(got, table, cache, *sides)
+
+
+def update_kernel(state_ref, got_ref, weight_ref, *refs, step, last):
     if last:
-        *weight_refs, out_ref = refs
+        (out_ref,) = refs
     else:
-        *weight_refs, out_ref, side_ref = refs
+        out_ref, side_ref = refs
         side_ref[...] = got_ref[:, :, HALF:]
     attended = jnp.concatenate(
         [
@@ -370,27 +312,23 @@
         axis=0,
     )
 
-    def act(weight_ref):
-        delta = jnp.dot(attended, weight_ref[...], preferred_element_type=f32)
-        pack(out_ref, state_ref[...] + delta)
-
-    pick(step, act, weight_refs)
-
-
-def update(state, got, weights, step):
-    rows, width = state.shape
+    delta = jnp.dot(attended, weight_ref[0, layer_of(step)], preferred_element_type=f32)
+    out_ref[...] = state_ref[...] + delta
+
+
+def update(state, got, weight, step):
     count, tree, total = got.shape
-    out_shape = (jax.ShapeDtypeStruct((rows, width + HEAD), jnp.int16),)
+    out_shape = (jax.ShapeDtypeStruct(state.shape, f32),)
     last = total == HALF
     if not last:
         out_shape += (jax.ShapeDtypeStruct((count, tree, total - HALF), bf16),)
     return pl.pallas_call(
         functools.partial(update_kernel, step=step, last=last),
         out_shape=out_shape,
-        in_specs=[VMEM] * (2 + len(weights)),
+        in_specs=[VMEM] * 3,
         out_specs=(VMEM,) * len(out_shape),
         compiler_params=PARAMS,
-    )(state, got, *weights)
+    )(state, got, weight)
 
 
 def exchange(value):
@@ -411,21 +349,18 @@
     mates = [(t, t ^ 1) for t in range(pieces.shape[0])]
     for step in range(kv_cache.shape[1]):
         if step:
-            pieces, state, sides = project(packed, mine, come, gain, weights_in, step)
-            (spread,) = attend(exchange(pieces), table, cache, step, sides)
+            pieces, sides = project(state, mine, come, gain, weights_in, step)
+            spread = attend(exchange(pieces), table, cache, step, (sides,))
         else:
-            spread, weight_out = attend(exchange(pieces), table, cache, step, weight=w_out)
-            weights_out = (weight_out,)
-        packed, *mine = update(state, exchange(spread), weights_out, step)
+            spread = attend(exchange(pieces), table, cache, step)
+        state, *mine = update(state, exchange(spread), w_out, step)
         if not step:
-            more_in, more_out = rest(w_qkv, w_out, packed)
-            weights_in += (more_in,)
-            weights_out += (more_out,)
-        packed = lax.ppermute(packed, "section", ring)
+            weights_in += (rest(w_qkv, state),)
+        state = lax.ppermute(state, "section", ring)
         if mine:
             (mine,) = mine
             come = lax.ppermute(mine, "tensor", mates)
-    return expand(packed).reshape(hidden_in.shape)
+    return state.reshape(hidden_in.shape)
 
 
 def solution(mesh):

time: 158 us -> 158 us (level)
  waiting for transfers between devices: 22.3 us -> 28 us
  Pallas kernels: 13.6 us -> 10.4 us
  blocking collectives: 119 us -> 116 us
    ppermute x4, waiting for transfers between devices: 10.4 us -> 15.5 us  [body(): state = lax.ppermute(state, 'section', ring)]
    all_to_all x8, blocking collectives: 119 us -> 116 us  [exchange(): return lax.all_to_all(value, 'tensor', 0, 0, tiled=True)]
    pallas_call x6 -> x5, Pallas kernels: 6.55 us -> 3.97 us  [the longest x4 2.24 us: attend(): pl.pallas_call(functools.partial(attend_kernel, step=step), out_shape=jax...]
  transfers between devices with their start and end apart: 7 -> 7, of which waited for: 7 -> 7; matrix products, arithmetic and copies ran while one was open for 0% -> 0% of each run, Pallas kernels for 2% -> 1%
where the time goes in v3:
time: 158 us; the launch traced here: 157 us
  blocking collectives  116 us (73%)
  waiting for transfers between devices  28 us (18%)
  Pallas kernels  10.4 us (7%)
  starting transfers between devices  2.19 us (1%)
    all_to_all x8, blocking collectives, exchange(): return lax.all_to_all(value, 'tensor', 0, 0, tiled=True)  116 us
    ppermute x4, waiting for transfers between devices, body(): state = lax.ppermute(state, 'section', ring)  15.5 us
    ppermute x3, waiting for transfers between devices, body(): come = lax.ppermute(mine, 'tensor', mates)  12.5 us
  transfers between devices with their start and end apart: 7, of which 7 were waited for; matrix products, arithmetic and copies ran while one was open for 0% of the time, Pallas kernels for 1%

profile of v3, /device:TPU:16, one launch (start us, length us, event | category | flops | bytes accessed | tf_op | source)
XLA Modules:
  0.0 157.2 jit_solution(6552260501740231277)
XLA Ops:
  0.0 2.6 %shard_map.82 = (bf16[8,16,1920]{2,1,0:T(8,128)(2,1)S(1)}, f32[64,1024]{1,0:T(8,128)S(1)}, f32[4,16,128]{2,1,0:T(8,128)S(1)}, f32[2,1024]{1,0:T(2,128)S(1)}, bf1...) custom-call(s32[4,16]{1,0:T(4,128)} %bitcast.7, s32[16,64]{1,0:T(8,128)} %bitcast.6, s32[64]{0:T(128)} %lengths_far.1, ...), custom_call_target="tpu_custom_call" | custom-call | tf_op jit(solution)/shard_map/pallas_call | solution.py:148
  2.6 25.1 %all_to_all.40.got_ref = bf16[8,16,1920]{2,1,0:T(8,128)(2,1)S(1)} all-to-all(bf16[8,16,1920]{2,1,0:T(8,128)(2,1)S(1)} %get-tuple-element.24), channel_id=1, replica_groups=mesh['dp'=2,'section'=16,'tensor'=8] {'tensor'}, dimensions={0} | all-to-all | bytes 983040 | tf_op jit(solution)/shard_map/all_to_all | solution.py:335
  27.7 0.6 shard_map.83
  28.2 12.9 %all_to_all.41.got_ref = bf16[8,16,1024]{2,1,0:T(8,128)(2,1)S(1)} all-to-all(bf16[8,16,1024]{2,1,0:T(8,128)(2,1)S(1)} %shard_map.83), channel_id=1, replica_groups=mesh['dp'=2,'section'=16,'tensor'=8] {'tensor'}, dimensions={0} | all-to-all | bytes 524288 | tf_op jit(solution)/shard_map/all_to_all | solution.py:335
  41.7 0.7 collective-permute-start.1
  42.4 1.7 %shard_map.85.refs_1_ = bf16[1024,1280]{1,0:T(8,128)(2,1)S(1)} custom-call(bf16[1,2,1024,1280]{3,2,1,0:T(8,128)(2,1)} %in_far.1, f32[64,1024]{1,0:T(8,128)S(1)} %get-tuple-element.27._), custom_call_target="tpu_custom_call" | custom-call | tf_op jit(solution)/shard_map/pallas_call | solution.py:181
  44.1 3.6 %collective-permute-done.1.come_ref = bf16[8,16,512]{2,1,0:T(8,128)(2,1)S(1)} collective-permute-done((bf16[8,16,512]{2,1,0:T(8,128)(2,1)S(1)}, bf16[8,16,512]{2,1,0:T(8,128)(2,1)S(1)}, u32[]{:S(2)}, u32[]{:S(2)}) %collective-permute-start.1) | collective-permute-done | bytes 131104 | tf_op jit(solution)/shard_map/ppermute | solution.py:362
  47.7 1.9 %collective-permute-done.state_ref = f32[64,1024]{1,0:T(8,128)S(1)} collective-permute-done((f32[64,1024]{1,0:T(8,128)S(1)}, f32[64,1024]{1,0:T(8,128)S(1)}, u32[]{:S(2)}, u32[]{:S(2)}) %collective-permute-start) | collective-permute-done | bytes 262176 | tf_op jit(solution)/shard_map/ppermute | solution.py:359
  49.6 0.6 shard_map.86
  50.3 12.8 %all_to_all.42.got_ref = bf16[8,16,896]{2,1,0:T(8,128)(2,1)S(1)} all-to-all(bf16[8,16,896]{2,1,0:T(8,128)(2,1)S(1)} %get-tuple-element.31), channel_id=1, replica_groups=mesh['dp'=2,'section'=16,'tensor'=8] {'tensor'}, dimensions={0} | all-to-all | bytes 458752 | tf_op jit(solution)/shard_map/all_to_all | solution.py:335
  63.6 12.9 %all_to_all.43.got_ref = bf16[8,16,1024]{2,1,0:T(8,128)(2,1)S(1)} all-to-all(bf16[8,16,1024]{2,1,0:T(8,128)(2,1)S(1)} %shard_map.87), channel_id=1, replica_groups=mesh['dp'=2,'section'=16,'tensor'=8] {'tensor'}, dimensions={0} | all-to-all | bytes 524288 | tf_op jit(solution)/shard_map/all_to_all | solution.py:335
  77.6 4.5 %collective-permute-done.3.come_ref = bf16[8,16,512]{2,1,0:T(8,128)(2,1)S(1)} collective-permute-done((bf16[8,16,512]{2,1,0:T(8,128)(2,1)S(1)}, bf16[8,16,512]{2,1,0:T(8,128)(2,1)S(1)}, u32[]{:S(2)}, u32[]{:S(2)}) %collective-permute-start.3) | collective-permute-done | bytes 131104 | tf_op jit(solution)/shard_map/ppermute | solution.py:362
  82.1 2.8 %collective-permute-done.2.state_ref = f32[64,1024]{1,0:T(8,128)S(1)} collective-permute-done((f32[64,1024]{1,0:T(8,128)S(1)}, f32[64,1024]{1,0:T(8,128)S(1)}, u32[]{:S(2)}, u32[]{:S(2)}) %collective-permute-start.2) | collective-permute-done | bytes 262176 | tf_op jit(solution)/shard_map/ppermute | solution.py:359
  85.0 0.6 shard_map.89
  85.6 13.4 %all_to_all.44.got_ref = bf16[8,16,896]{2,1,0:T(8,128)(2,1)S(1)} all-to-all(bf16[8,16,896]{2,1,0:T(8,128)(2,1)S(1)} %get-tuple-element.35), channel_id=1, replica_groups=mesh['dp'=2,'section'=16,'tensor'=8] {'tensor'}, dimensions={0} | all-to-all | bytes 458752 | tf_op jit(solution)/shard_map/all_to_all | solution.py:335
  99.5 12.9 %all_to_all.45.got_ref = bf16[8,16,1024]{2,1,0:T(8,128)(2,1)S(1)} all-to-all(bf16[8,16,1024]{2,1,0:T(8,128)(2,1)S(1)} %shard_map.90), channel_id=1, replica_groups=mesh['dp'=2,'section'=16,'tensor'=8] {'tensor'}, dimensions={0} | all-to-all | bytes 524288 | tf_op jit(solution)/shard_map/all_to_all | solution.py:335
  113.0 0.7 collective-permute-start.5
  113.7 4.4 %collective-permute-done.5.come_ref = bf16[8,16,512]{2,1,0:T(8,128)(2,1)S(1)} collective-permute-done((bf16[8,16,512]{2,1,0:T(8,128)(2,1)S(1)}, bf16[8,16,512]{2,1,0:T(8,128)(2,1)S(1)}, u32[]{:S(2)}, u32[]{:S(2)}) %collective-permute-start.5) | collective-permute-done | bytes 131104 | tf_op jit(solution)/shard_map/ppermute | solution.py:362
  118.1 2.8 %collective-permute-done.4.state_ref = f32[64,1024]{1,0:T(8,128)S(1)} collective-permute-done((f32[64,1024]{1,0:T(8,128)S(1)}, f32[64,1024]{1,0:T(8,128)S(1)}, u32[]{:S(2)}, u32[]{:S(2)}) %collective-permute-start.4) | collective-permute-done | bytes 262176 | tf_op jit(solution)/shard_map/ppermute | solution.py:359
  120.9 0.6 shard_map.92
  121.5 14.1 %all_to_all.46.got_ref = bf16[8,16,896]{2,1,0:T(8,128)(2,1)S(1)} all-to-all(bf16[8,16,896]{2,1,0:T(8,128)(2,1)S(1)} %get-tuple-element.39), channel_id=1, replica_groups=mesh['dp'=2,'section'=16,'tensor'=8] {'tensor'}, dimensions={0} | all-to-all | bytes 458752 | tf_op jit(solution)/shard_map/all_to_all | solution.py:335
  136.2 11.8 %all_to_all.47.got_ref = bf16[8,16,512]{2,1,0:T(8,128)(2,1)S(1)} all-to-all(bf16[8,16,512]{2,1,0:T(8,128)(2,1)S(1)} %shard_map.93), channel_id=1, replica_groups=mesh['dp'=2,'section'=16,'tensor'=8] {'tensor'}, dimensions={0} | all-to-all | bytes 262144 | tf_op jit(solution)/shard_map/all_to_all | solution.py:335
  148.6 7.9 %collective-permute-done.6 = f32[64,1024]{1,0:T(8,128)S(1)} collective-permute-done((f32[64,1024]{1,0:T(8,128)S(1)}, f32[64,1024]{1,0:T(8,128)S(1)}, u32[]{:S(2)}, u32[]{:S(2)}) %collective-permute-start.6) | collective-permute-done | bytes 262176 | tf_op jit(solution)/shard_map/ppermute | solution.py:359
  156.5 0.7 copy.10
  (14 shorter events, 4.5 us)
Async XLA Ops:
  0.0 41.1 %copy-start = (bf16[1,2,1024,1024]{3,2,1,0:T(8,128)(2,1)S(1)}, bf16[1,2,1024,1024]{3,2,1,0:T(8,128)(2,1)}, u32[]{:S(2)}) copy-start(bf16[1,2,1024,1024]{3,2,1,0:T(8,128)(2,1)} %weight_ref.7) | copy-start | bytes 12582916
  41.6 8.0 %collective-permute-start = (f32[64,1024]{1,0:T(8,128)S(1)}, f32[64,1024]{1,0:T(8,128)S(1)}, u32[]{:S(2)}, u32[]{:S(2)}) collective-permute-start(f32[64,1024]{1,0:T(8,128)S(1)} %get-tuple-element.27._), channel_id=1, source_target_pairs={{0,8},{8,16},{16,24},{24,32},{32,40},{40,48},{48,56},{56,64},{64,7... | collective-permute-start | bytes 786440 | tf_op jit(solution)/shard_map/ppermute | solution.py:359
  41.7 6.0 %collective-permute-start.1 = (bf16[8,16,512]{2,1,0:T(8,128)(2,1)S(1)}, bf16[8,16,512]{2,1,0:T(8,128)(2,1)S(1)}, u32[]{:S(2)}, u32[]{:S(2)}) collective-permute-start(bf16[8,16,512]{2,1,0:T(8,128)(2,1)S(1)} %get-tuple-element.28.mine_ref), channel_id=1, source_target_pairs={{0,1},{1,0},{2,3},{3,2},{4,5},{5,4},{6,7},{7,6},{8,9},{9,8},{10,11... | collective-permute-start | bytes 393224 | tf_op jit(solution)/shard_map/ppermute | solution.py:362
  77.0 8.0 %collective-permute-start.2 = (f32[64,1024]{1,0:T(8,128)S(1)}, f32[64,1024]{1,0:T(8,128)S(1)}, u32[]{:S(2)}, u32[]{:S(2)}) collective-permute-start(f32[64,1024]{1,0:T(8,128)S(1)} %get-tuple-element.33), channel_id=1, source_target_pairs={{0,8},{8,16},{16,24},{24,32},{32,40},{40,48},{48,56},{56,64},{64,7... | collective-permute-start | bytes 786440 | tf_op jit(solution)/shard_map/ppermute | solution.py:359
  77.1 5.1 %collective-permute-start.3 = (bf16[8,16,512]{2,1,0:T(8,128)(2,1)S(1)}, bf16[8,16,512]{2,1,0:T(8,128)(2,1)S(1)}, u32[]{:S(2)}, u32[]{:S(2)}) collective-permute-start(bf16[8,16,512]{2,1,0:T(8,128)(2,1)S(1)} %get-tuple-element.34.mine_ref), channel_id=1, source_target_pairs={{0,1},{1,0},{2,3},{3,2},{4,5},{5,4},{6,7},{7,6},{8,9},{9,8},{10,11... | collective-permute-start | bytes 393224 | tf_op jit(solution)/shard_map/ppermute | solution.py:362
  112.9 8.0 %collective-permute-start.4 = (f32[64,1024]{1,0:T(8,128)S(1)}, f32[64,1024]{1,0:T(8,128)S(1)}, u32[]{:S(2)}, u32[]{:S(2)}) collective-permute-start(f32[64,1024]{1,0:T(8,128)S(1)} %get-tuple-element.37), channel_id=1, source_target_pairs={{0,8},{8,16},{16,24},{24,32},{32,40},{40,48},{48,56},{56,64},{64,7... | collective-permute-start | bytes 786440 | tf_op jit(solution)/shard_map/ppermute | solution.py:359
  113.0 5.1 %collective-permute-start.5 = (bf16[8,16,512]{2,1,0:T(8,128)(2,1)S(1)}, bf16[8,16,512]{2,1,0:T(8,128)(2,1)S(1)}, u32[]{:S(2)}, u32[]{:S(2)}) collective-permute-start(bf16[8,16,512]{2,1,0:T(8,128)(2,1)S(1)} %get-tuple-element.38.mine_ref), channel_id=1, source_target_pairs={{0,1},{1,0},{2,3},{3,2},{4,5},{5,4},{6,7},{7,6},{8,9},{9,8},{10,11... | collective-permute-start | bytes 393224 | tf_op jit(solution)/shard_map/ppermute | solution.py:362
  148.5 8.0 %collective-permute-start.6 = (f32[64,1024]{1,0:T(8,128)S(1)}, f32[64,1024]{1,0:T(8,128)S(1)}, u32[]{:S(2)}, u32[]{:S(2)}) collective-permute-start(f32[64,1024]{1,0:T(8,128)S(1)} %shard_map.94), channel_id=1, source_target_pairs={{0,8},{8,16},{16,24},{24,32},{32,40},{40,48},{48,56},{56,64},{64,7... | collective-permute-start | bytes 786440 | tf_op jit(solution)/shard_map/ppermute | solution.py:359

commit v4 on v3

--- a/solution.py
+++ b/solution.py
@@ -196,11 +196,8 @@
         pl.when(which == index)(functools.partial(act, layer))
 
 
-def project_kernel(state_ref, mine_ref, come_ref, gain_ref, *refs, step):
-    *weight_refs, out_ref, sides_ref = refs
-    side = lax.rem(lax.axis_index("tensor"), 2)
-    sides_ref[side] = mine_ref[...]
-    sides_ref[1 - side] = come_ref[...]
+def project_kernel(state_ref, gain_ref, *refs, step):
+    *weight_refs, out_ref = refs
     state = state_ref[...]
     scaled = (state * gain_ref[pl.ds(layer_of(step), 1), :]).astype(bf16)
 
@@ -211,17 +208,14 @@
     pick(step, act, weight_refs)
 
 
-def project(state, mine, come, gain, weights, step):
+def project(state, gain, weights, step):
     return pl.pallas_call(
         functools.partial(project_kernel, step=step),
-        out_shape=(
-            jax.ShapeDtypeStruct((mine.shape[0], TREE, PIECE), bf16),
-            jax.ShapeDtypeStruct((2,) + mine.shape, bf16),
-        ),
-        in_specs=[VMEM] * (4 + len(weights)),
-        out_specs=(VMEM,) * 2,
-        compiler_params=PARAMS,
-    )(state, mine, come, gain, *weights)
+        out_shape=jax.ShapeDtypeStruct((2 * state.shape[0] // TREE, TREE, PIECE), bf16),
+        in_specs=[VMEM] * (2 + len(weights)),
+        out_specs=VMEM,
+        compiler_params=PARAMS,
+    )(state, gain, *weights)
 
 
 def attend_kernel(got_ref, table_ref, cache_ref, *refs, step):
@@ -237,13 +231,14 @@
     tree_keys = projected[:, HALF : HALF + HEAD]
     tree_values = projected[:, HALF + HEAD :]
     if step:
+        mine_ref, come_ref = sides_ref
         blocks = [
             [
-                sides_ref[0][side, piece, :, start : start + HEAD]
-                for piece in range(sides_ref[0].shape[1])
-                for start in range(0, sides_ref[0].shape[3], HEAD)
+                side_ref[piece, :, start : start + HEAD]
+                for piece in range(side_ref.shape[0])
+                for start in range(0, side_ref.shape[2], HEAD)
             ]
-            for side in range(2)
+            for side_ref in (mine_ref, come_ref)
         ]
     else:
         blocks = [
@@ -255,6 +250,9 @@
             for side in range(2)
         ]
     keys, values = (jnp.concatenate(block, axis=0) for block in blocks)
+    if step:
+        swapped = lax.rem(lax.axis_index("tensor"), 2) == 1
+        keys, values = jnp.where(swapped, values, keys), jnp.where(swapped, keys, values)
     contract = (((1,), (1,)), ((), ()))
     scaling = HEAD ** (-0.5)
     scores = lax.dot_general(queries, keys, contract, preferred_element_type=f32)
@@ -349,8 +347,9 @@
     mates = [(t, t ^ 1) for t in range(pieces.shape[0])]
     for step in range(kv_cache.shape[1]):
         if step:
-            pieces, sides = project(state, mine, come, gain, weights_in, step)
-            spread = attend(exchange(pieces), table, cache, step, (sides,))
+            pieces = project(state, gain, weights_in, step)
+            pieces, come = lax.optimization_barrier((pieces, come))
+            spread = attend(exchange(pieces), table, cache, step, (mine, come))
         else:
             spread = attend(exchange(pieces), table, cache, step)
         state, *mine = update(state, exchange(spread), w_out, step)

time: 158 us -> 155 us (0.981)
  blocking collectives: 116 us -> 113 us
    ppermute x4, waiting for transfers between devices: 15.5 us -> 28.6 us  [body(): state = lax.ppermute(state, 'section', ring)]
    ppermute x3, waiting for transfers between devices: 12.5 us -> 0.01 us  [body(): come = lax.ppermute(mine, 'tensor', mates)]
    all_to_all x8, blocking collectives: 116 us -> 113 us  [exchange(): return lax.all_to_all(value, 'tensor', 0, 0, tiled=True)]
  transfers between devices with their start and end apart: 7 -> 7, of which waited for: 7 -> 4; matrix products, arithmetic and copies ran while one was open for 0% -> 0% of each run, Pallas kernels for 1% -> 2%
where the time goes in v4:
time: 155 us; the launch traced here: 154 us
  blocking collectives  113 us (73%)
  waiting for transfers between devices  28.6 us (18%)
  Pallas kernels  10.3 us (7%)
  starting transfers between devices  1.58 us (1%)
    all_to_all x8, blocking collectives, exchange(): return lax.all_to_all(value, 'tensor', 0, 0, tiled=True)  113 us
    ppermute x4, waiting for transfers between devices, body(): state = lax.ppermute(state, 'section', ring)  28.6 us
  transfers between devices with their start and end apart: 7, of which 4 were waited for; matrix products, arithmetic and copies ran while one was open for 0% of the time, Pallas kernels for 2%

profile of v4, /device:TPU:16, one launch (start us, length us, event | category | flops | bytes accessed | tf_op | source)
XLA Modules:
  0.0 154.2 jit_solution(4642689698261279353)
XLA Ops:
  0.0 2.6 %shard_map.82 = (bf16[8,16,1920]{2,1,0:T(8,128)(2,1)S(1)}, f32[64,1024]{1,0:T(8,128)S(1)}, f32[4,16,128]{2,1,0:T(8,128)S(1)}, f32[2,1024]{1,0:T(2,128)S(1)}, bf1...) custom-call(s32[4,16]{1,0:T(4,128)} %bitcast.7, s32[16,64]{1,0:T(8,128)} %bitcast.6, s32[64]{0:T(128)} %lengths_far.1, ...), custom_call_target="tpu_custom_call" | custom-call | tf_op jit(solution)/shard_map/pallas_call | solution.py:148
  2.6 25.1 %all_to_all.40.got_ref = bf16[8,16,1920]{2,1,0:T(8,128)(2,1)S(1)} all-to-all(bf16[8,16,1920]{2,1,0:T(8,128)(2,1)S(1)} %get-tuple-element.24), channel_id=1, replica_groups=mesh['dp'=2,'section'=16,'tensor'=8] {'tensor'}, dimensions={0} | all-to-all | bytes 983040 | tf_op jit(solution)/shard_map/all_to_all | solution.py:333
  27.7 0.6 shard_map.83
  28.2 12.9 %all_to_all.41.got_ref = bf16[8,16,1024]{2,1,0:T(8,128)(2,1)S(1)} all-to-all(bf16[8,16,1024]{2,1,0:T(8,128)(2,1)S(1)} %shard_map.83), channel_id=1, replica_groups=mesh['dp'=2,'section'=16,'tensor'=8] {'tensor'}, dimensions={0} | all-to-all | bytes 524288 | tf_op jit(solution)/shard_map/all_to_all | solution.py:333
  41.1 0.5 shard_map.84
  41.7 0.7 collective-permute-start.1
  42.4 1.7 %shard_map.85.refs_1_ = bf16[1024,1280]{1,0:T(8,128)(2,1)S(1)} custom-call(bf16[1,2,1024,1280]{3,2,1,0:T(8,128)(2,1)} %in_far.1, f32[64,1024]{1,0:T(8,128)S(1)} %get-tuple-element.27._), custom_call_target="tpu_custom_call" | custom-call | tf_op jit(solution)/shard_map/pallas_call | solution.py:181
  44.1 5.5 %collective-permute-done.state_ref = f32[64,1024]{1,0:T(8,128)S(1)} collective-permute-done((f32[64,1024]{1,0:T(8,128)S(1)}, f32[64,1024]{1,0:T(8,128)S(1)}, u32[]{:S(2)}, u32[]{:S(2)}) %collective-permute-start) | collective-permute-done | bytes 262176 | tf_op jit(solution)/shard_map/ppermute | solution.py:358
  49.6 0.6 shard_map.86
  50.2 12.5 %all_to_all.42.got_ref = bf16[8,16,896]{2,1,0:T(8,128)(2,1)S(1)} all-to-all(bf16[8,16,896]{2,1,0:T(8,128)(2,1)S(1)} %shard_map.86), channel_id=1, replica_groups=mesh['dp'=2,'section'=16,'tensor'=8] {'tensor'}, dimensions={0} | all-to-all | bytes 458752 | tf_op jit(solution)/shard_map/all_to_all | solution.py:333
  62.8 0.6 shard_map.87
  63.3 12.9 %all_to_all.43.got_ref = bf16[8,16,1024]{2,1,0:T(8,128)(2,1)S(1)} all-to-all(bf16[8,16,1024]{2,1,0:T(8,128)(2,1)S(1)} %shard_map.87), channel_id=1, replica_groups=mesh['dp'=2,'section'=16,'tensor'=8] {'tensor'}, dimensions={0} | all-to-all | bytes 524288 | tf_op jit(solution)/shard_map/all_to_all | solution.py:333
  77.1 7.6 %collective-permute-done.2.state_ref = f32[64,1024]{1,0:T(8,128)S(1)} collective-permute-done((f32[64,1024]{1,0:T(8,128)S(1)}, f32[64,1024]{1,0:T(8,128)S(1)}, u32[]{:S(2)}, u32[]{:S(2)}) %collective-permute-start.2) | collective-permute-done | bytes 262176 | tf_op jit(solution)/shard_map/ppermute | solution.py:358
  84.7 0.6 shard_map.89
  85.3 12.5 %all_to_all.44.got_ref = bf16[8,16,896]{2,1,0:T(8,128)(2,1)S(1)} all-to-all(bf16[8,16,896]{2,1,0:T(8,128)(2,1)S(1)} %shard_map.89), channel_id=1, replica_groups=mesh['dp'=2,'section'=16,'tensor'=8] {'tensor'}, dimensions={0} | all-to-all | bytes 458752 | tf_op jit(solution)/shard_map/all_to_all | solution.py:333
  97.9 0.6 shard_map.90
  98.4 12.9 %all_to_all.45.got_ref = bf16[8,16,1024]{2,1,0:T(8,128)(2,1)S(1)} all-to-all(bf16[8,16,1024]{2,1,0:T(8,128)(2,1)S(1)} %shard_map.90), channel_id=1, replica_groups=mesh['dp'=2,'section'=16,'tensor'=8] {'tensor'}, dimensions={0} | all-to-all | bytes 524288 | tf_op jit(solution)/shard_map/all_to_all | solution.py:333
  112.2 7.6 %collective-permute-done.4.state_ref = f32[64,1024]{1,0:T(8,128)S(1)} collective-permute-done((f32[64,1024]{1,0:T(8,128)S(1)}, f32[64,1024]{1,0:T(8,128)S(1)}, u32[]{:S(2)}, u32[]{:S(2)}) %collective-permute-start.4) | collective-permute-done | bytes 262176 | tf_op jit(solution)/shard_map/ppermute | solution.py:358
  119.8 0.6 shard_map.92
  120.4 12.5 %all_to_all.46.got_ref = bf16[8,16,896]{2,1,0:T(8,128)(2,1)S(1)} all-to-all(bf16[8,16,896]{2,1,0:T(8,128)(2,1)S(1)} %shard_map.92), channel_id=1, replica_groups=mesh['dp'=2,'section'=16,'tensor'=8] {'tensor'}, dimensions={0} | all-to-all | bytes 458752 | tf_op jit(solution)/shard_map/all_to_all | solution.py:333
  133.0 0.6 shard_map.93
  133.5 11.5 %all_to_all.47.got_ref = bf16[8,16,512]{2,1,0:T(8,128)(2,1)S(1)} all-to-all(bf16[8,16,512]{2,1,0:T(8,128)(2,1)S(1)} %shard_map.93), channel_id=1, replica_groups=mesh['dp'=2,'section'=16,'tensor'=8] {'tensor'}, dimensions={0} | all-to-all | bytes 262144 | tf_op jit(solution)/shard_map/all_to_all | solution.py:333
  145.6 7.9 %collective-permute-done.6 = f32[64,1024]{1,0:T(8,128)S(1)} collective-permute-done((f32[64,1024]{1,0:T(8,128)S(1)}, f32[64,1024]{1,0:T(8,128)S(1)}, u32[]{:S(2)}, u32[]{:S(2)}) %collective-permute-start.6) | collective-permute-done | bytes 262176 | tf_op jit(solution)/shard_map/ppermute | solution.py:358
  153.5 0.7 copy.10
  (14 shorter events, 2.4 us)
Async XLA Ops:
  0.0 41.1 %copy-start = (bf16[1,2,1024,1024]{3,2,1,0:T(8,128)(2,1)S(1)}, bf16[1,2,1024,1024]{3,2,1,0:T(8,128)(2,1)}, u32[]{:S(2)}) copy-start(bf16[1,2,1024,1024]{3,2,1,0:T(8,128)(2,1)} %weight_ref.7) | copy-start | bytes 12582916
  41.6 8.0 %collective-permute-start = (f32[64,1024]{1,0:T(8,128)S(1)}, f32[64,1024]{1,0:T(8,128)S(1)}, u32[]{:S(2)}, u32[]{:S(2)}) collective-permute-start(f32[64,1024]{1,0:T(8,128)S(1)} %get-tuple-element.27._), channel_id=1, source_target_pairs={{0,8},{8,16},{16,24},{24,32},{32,40},{40,48},{48,56},{56,64},{64,7... | collective-permute-start | bytes 786440 | tf_op jit(solution)/shard_map/ppermute | solution.py:358
  41.7 8.5 %collective-permute-start.1 = (bf16[8,16,512]{2,1,0:T(8,128)(2,1)S(1)}, bf16[8,16,512]{2,1,0:T(8,128)(2,1)S(1)}, u32[]{:S(2)}, u32[]{:S(2)}) collective-permute-start(bf16[8,16,512]{2,1,0:T(8,128)(2,1)S(1)} %get-tuple-element.30.refs_0_), channel_id=1, source_target_pairs={{0,1},{1,0},{2,3},{3,2},{4,5},{5,4},{6,7},{7,6},{8,9},{9,8},{10,11... | collective-permute-start | bytes 393224 | tf_op jit(solution)/shard_map/ppermute | solution.py:361
  76.7 8.0 %collective-permute-start.2 = (f32[64,1024]{1,0:T(8,128)S(1)}, f32[64,1024]{1,0:T(8,128)S(1)}, u32[]{:S(2)}, u32[]{:S(2)}) collective-permute-start(f32[64,1024]{1,0:T(8,128)S(1)} %get-tuple-element.33), channel_id=1, source_target_pairs={{0,8},{8,16},{16,24},{24,32},{32,40},{40,48},{48,56},{56,64},{64,7... | collective-permute-start | bytes 786440 | tf_op jit(solution)/shard_map/ppermute | solution.py:358
  76.8 8.5 %collective-permute-start.3 = (bf16[8,16,512]{2,1,0:T(8,128)(2,1)S(1)}, bf16[8,16,512]{2,1,0:T(8,128)(2,1)S(1)}, u32[]{:S(2)}, u32[]{:S(2)}) collective-permute-start(bf16[8,16,512]{2,1,0:T(8,128)(2,1)S(1)} %get-tuple-element.34.refs_0_), channel_id=1, source_target_pairs={{0,1},{1,0},{2,3},{3,2},{4,5},{5,4},{6,7},{7,6},{8,9},{9,8},{10,11... | collective-permute-start | bytes 393224 | tf_op jit(solution)/shard_map/ppermute | solution.py:361
  111.8 8.0 %collective-permute-start.4 = (f32[64,1024]{1,0:T(8,128)S(1)}, f32[64,1024]{1,0:T(8,128)S(1)}, u32[]{:S(2)}, u32[]{:S(2)}) collective-permute-start(f32[64,1024]{1,0:T(8,128)S(1)} %get-tuple-element.37), channel_id=1, source_target_pairs={{0,8},{8,16},{16,24},{24,32},{32,40},{40,48},{48,56},{56,64},{64,7... | collective-permute-start | bytes 786440 | tf_op jit(solution)/shard_map/ppermute | solution.py:358
  111.9 8.5 %collective-permute-start.5 = (bf16[8,16,512]{2,1,0:T(8,128)(2,1)S(1)}, bf16[8,16,512]{2,1,0:T(8,128)(2,1)S(1)}, u32[]{:S(2)}, u32[]{:S(2)}) collective-permute-start(bf16[8,16,512]{2,1,0:T(8,128)(2,1)S(1)} %get-tuple-element.38.refs_0_), channel_id=1, source_target_pairs={{0,1},{1,0},{2,3},{3,2},{4,5},{5,4},{6,7},{7,6},{8,9},{9,8},{10,11... | collective-permute-start | bytes 393224 | tf_op jit(solution)/shard_map/ppermute | solution.py:361
  145.5 8.0 %collective-permute-start.6 = (f32[64,1024]{1,0:T(8,128)S(1)}, f32[64,1024]{1,0:T(8,128)S(1)}, u32[]{:S(2)}, u32[]{:S(2)}) collective-permute-start(f32[64,1024]{1,0:T(8,128)S(1)} %shard_map.94), channel_id=1, source_target_pairs={{0,8},{8,16},{16,24},{24,32},{32,40},{40,48},{48,56},{56,64},{64,7... | collective-permute-start | bytes 786440 | tf_op jit(solution)/shard_map/ppermute | solution.py:358

commit v5 on v4

--- a/solution.py
+++ b/solution.py
@@ -22,6 +22,8 @@
 MIX = 768
 PIECE = 896
 CHUNKS = 8
+TOP = 125.0
+PARTS = 1
 VMEM_LIMIT = 16 * 1024 * 1024
 
 VMEM = pl.BlockSpec(memory_space=pltpu.VMEM)
@@ -87,8 +89,8 @@
 
 def first_kernel(
     assign_far, parents_far, lengths_far, state_far, gain_far, weight_far, cache_far,
-    out_ref, state_ref, table_ref, gain_ref, weight_ref, cache_ref,
-    assign_ref, parents_ref, lengths_ref, rows, sems, more,
+    out_ref, state_ref, table_ref, gain_ref, cache_ref,
+    assign_ref, parents_ref, lengths_ref, rows, weight_ref, sems, more,
 ):
     weight_copies = loads(weight_far.at[0, 0], weight_ref, sems)
     other = [
@@ -152,16 +154,16 @@
             pltpu.VMEM((slots * tree, width), f32),
             pltpu.VMEM((steps, TREE, HEAD), f32),
             pltpu.VMEM(gain.shape[1:], f32),
-            pltpu.VMEM(weight.shape[2:], bf16),
             pltpu.VMEM(cache.shape[1:], bf16),
         ),
         in_specs=[FAR] * 7,
-        out_specs=(VMEM,) * 6,
+        out_specs=(VMEM,) * 5,
         scratch_shapes=[
             pltpu.SMEM(assign.shape[::-1], jnp.int32),
             pltpu.SMEM(parents.shape[::-1], jnp.int32),
             pltpu.SMEM(lengths.shape, jnp.int32),
             pltpu.VMEM((steps, TREE, HEAD), f32),
+            pltpu.VMEM(weight.shape[2:], bf16),
             pltpu.SemaphoreType.DMA((CHUNKS,)),
             pltpu.SemaphoreType.DMA((6,)),
         ],
@@ -169,53 +171,66 @@
     )(*map(far, (assign.T, parents.T, lengths, rows, gain, weight, cache)))
 
 
-def rest_kernel(in_far, _, in_ref, sems):
-    copies = loads(in_far.at[0, 1], in_ref, sems)
-    for copy in copies:
-        copy.start()
-    for copy in copies:
-        copy.wait()
-
-
-def rest(weight_in, after):
-    return pl.pallas_call(
-        rest_kernel,
-        out_shape=pltpu.VMEM(weight_in.shape[2:], bf16),
-        in_specs=[FAR, VMEM],
+def unit_of(power):
+    return jnp.exp2(power) / jnp.where(power < TOP, 32767.0, 4095.0)
+
+
+def pack(packed_ref, state):
+    width = state.shape[1]
+    peak = jnp.max(jnp.abs(state), axis=-1, keepdims=True)
+    power = jnp.clip(jnp.ceil(jnp.log2(jnp.maximum(peak, 1e-37))), -TOP, TOP)
+    ratio = state * jnp.exp2(-power) * jnp.where(power < TOP, 32767.0, 4095.0)
+    steps = jnp.clip(jnp.round(ratio), -32767.0, 32767.0)
+    packed_ref[:, :width] = steps.astype(jnp.int32).astype(jnp.int16)
+    powers = jnp.broadcast_to(power.astype(jnp.int32), (state.shape[0], HEAD))
+    packed_ref[:, width:] = powers.astype(jnp.int16)
+
+
+def unpack(packed_ref):
+    width = packed_ref.shape[1] - HEAD
+    power = packed_ref[:, width:].astype(jnp.int32).astype(f32)[:, :1]
+    return packed_ref[:, :width].astype(jnp.int32).astype(f32) * unit_of(power)
+
+
+def expand_kernel(*refs):
+    *packed_refs, out_ref = refs
+    out_ref[...] = jnp.concatenate([unpack(packed_ref) for packed_ref in packed_refs], axis=0)
+
+
+def expand(packed):
+    rows, width = packed[0].shape
+    return pl.pallas_call(
+        expand_kernel,
+        out_shape=jax.ShapeDtypeStruct((rows * len(packed), width - HEAD), f32),
+        in_specs=[VMEM] * len(packed),
         out_specs=VMEM,
-        scratch_shapes=[pltpu.SemaphoreType.DMA((CHUNKS,))],
-        compiler_params=PARAMS,
-    )(far(weight_in), after)
-
-
-def pick(step, act, layers):
-    if len(layers) == 1:
-        return act(layers[0])
+        compiler_params=PARAMS,
+    )(*packed)
+
+
+def project_kernel(*refs, step):
+    *packed_refs, gain_ref, weight_ref, out_ref, state_ref = refs
+    state = jnp.concatenate([unpack(packed_ref) for packed_ref in packed_refs], axis=0)
+    state_ref[...] = state
     which = layer_of(step)
-    for index, layer in enumerate(layers):
-        pl.when(which == index)(functools.partial(act, layer))
-
-
-def project_kernel(state_ref, gain_ref, *refs, step):
-    *weight_refs, out_ref = refs
-    state = state_ref[...]
-    scaled = (state * gain_ref[pl.ds(layer_of(step), 1), :]).astype(bf16)
-
-    def act(weight_ref):
-        raw = jnp.dot(scaled, weight_ref[...], preferred_element_type=f32)
-        write_pieces(out_ref, raw, state)
-
-    pick(step, act, weight_refs)
-
-
-def project(state, gain, weights, step):
+    scaled = (state * gain_ref[pl.ds(which, 1), :]).astype(bf16)
+    raw = jnp.dot(scaled, weight_ref[0, which], preferred_element_type=f32)
+    write_pieces(out_ref, raw, state)
+
+
+def project(packed, gain, weight, step):
+    rows, width = packed[0].shape
+    rows *= len(packed)
     return pl.pallas_call(
         functools.partial(project_kernel, step=step),
-        out_shape=jax.ShapeDtypeStruct((2 * state.shape[0] // TREE, TREE, PIECE), bf16),
-        in_specs=[VMEM] * (2 + len(weights)),
-        out_specs=VMEM,
-        compiler_params=PARAMS,
-    )(state, gain, *weights)
+        out_shape=(
+            jax.ShapeDtypeStruct((2 * rows // TREE, TREE, PIECE), bf16),
+            jax.ShapeDtypeStruct((rows, width - HEAD), f32),
+        ),
+        in_specs=[VMEM] * (2 + len(packed)),
+        out_specs=(VMEM,) * 2,
+        compiler_params=PARAMS,
+    )(*packed, gain, weight)
 
 
 def attend_kernel(got_ref, table_ref, cache_ref, *refs, step):
@@ -298,9 +313,9 @@
 
 def update_kernel(state_ref, got_ref, weight_ref, *refs, step, last):
     if last:
-        (out_ref,) = refs
+        out_refs = refs
     else:
-        out_ref, side_ref = refs
+        *out_refs, side_ref = refs
         side_ref[...] = got_ref[:, :, HALF:]
     attended = jnp.concatenate(
         [
@@ -311,12 +326,16 @@
     )
 
     delta = jnp.dot(attended, weight_ref[0, layer_of(step)], preferred_element_type=f32)
-    out_ref[...] = state_ref[...] + delta
+    state = state_ref[...] + delta
+    rows = out_refs[0].shape[0]
+    for part, out_ref in enumerate(out_refs):
+        pack(out_ref, state[part * rows : (part + 1) * rows])
 
 
 def update(state, got, weight, step):
+    rows, width = state.shape
     count, tree, total = got.shape
-    out_shape = (jax.ShapeDtypeStruct(state.shape, f32),)
+    out_shape = (jax.ShapeDtypeStruct((rows // PARTS, width + HEAD), jnp.int16),) * PARTS
     last = total == HALF
     if not last:
         out_shape += (jax.ShapeDtypeStruct((count, tree, total - HALF), bf16),)
@@ -340,26 +359,24 @@
 def body(hidden_in, norm_gain, w_qkv, w_out, kv_cache, parents, lengths, assign):
     sections = lax.axis_size("section")
     ring = [(s, (s + 1) % sections) for s in range(sections)]
-    pieces, state, table, gain, weight_in, cache = first(
+    pieces, state, table, gain, cache = first(
         assign, parents, lengths, hidden_in, norm_gain, w_qkv, kv_cache
     )
-    weights_in = (weight_in,)
     mates = [(t, t ^ 1) for t in range(pieces.shape[0])]
     for step in range(kv_cache.shape[1]):
         if step:
-            pieces = project(state, gain, weights_in, step)
+            pieces, state = project(packed, gain, w_qkv, step)
             pieces, come = lax.optimization_barrier((pieces, come))
             spread = attend(exchange(pieces), table, cache, step, (mine, come))
         else:
             spread = attend(exchange(pieces), table, cache, step)
-        state, *mine = update(state, exchange(spread), w_out, step)
-        if not step:
-            weights_in += (rest(w_qkv, state),)
-        state = lax.ppermute(state, "section", ring)
-        if mine:
-            (mine,) = mine
+        outs = update(state, exchange(spread), w_out, step)
+        parts = [lax.ppermute(part, "section", ring) for part in jnp.split(outs[0], [48])]
+        packed = [jnp.concatenate(parts)]
+        if len(outs) > 1:
+            mine = outs[1]
             come = lax.ppermute(mine, "tensor", mates)
-    return state.reshape(hidden_in.shape)
+    return expand(packed).reshape(hidden_in.shape)
 
 
 def solution(mesh):

time: 155 us -> 152 us (0.981)
  waiting for transfers between devices: 28.6 us -> 19.2 us
  starting transfers between devices: 1.58 us -> 7.73 us
    ppermute x4 -> x8, waiting for transfers between devices: 28.6 us -> 19.2 us  [body(): lax.ppermute(part, 'section', ring)]
    ppermute x4 -> x8, starting transfers between devices: 0.33 us -> 6.03 us  [body(): lax.ppermute(part, 'section', ring)]
  transfers between devices with their start and end apart: 7 -> 11, of which waited for: 4 -> 4; matrix products, arithmetic and copies ran while one was open for 0% -> 0% of each run, Pallas kernels for 2% -> 1%
where the time goes in v5:
time: 152 us
  blocking collectives  114 us (75%)
  waiting for transfers between devices  19.2 us (13%)
  Pallas kernels  10 us (7%)
  starting transfers between devices  7.73 us (5%)
    all_to_all x8, blocking collectives, exchange(): return lax.all_to_all(value, 'tensor', 0, 0, tiled=True)  114 us
    ppermute x8, waiting for transfers between devices, body(): lax.ppermute(part, 'section', ring)  19.2 us
    ppermute x8, starting transfers between devices, body(): lax.ppermute(part, 'section', ring)  6.03 us
  transfers between devices with their start and end apart: 11, of which 4 were waited for; matrix products, arithmetic and copies ran while one was open for 0% of the time, Pallas kernels for 1%

profile of v5, /device:TPU:16, one launch (start us, length us, event | category | flops | bytes accessed | tf_op | source)
XLA Modules:
  0.0 151.6 jit_solution(8876631414510326777)
XLA Ops:
  0.0 2.6 %shard_map.82 = (bf16[8,16,1920]{2,1,0:T(8,128)(2,1)S(1)}, f32[64,1024]{1,0:T(8,128)S(1)}, f32[4,16,128]{2,1,0:T(8,128)S(1)}, f32[2,1024]{1,0:T(2,128)S(1)}, bf16[4,4,64,256]{3,2,1,0:T(8,128)(2,1)S(1)}) custom-call(s32[4,16]{1,0:T(4,128)} %bitcast.6, s32[16,64]{1,0:T(8,128)} %bitcast.5, s32[64]{0:T(128)} %lengths_far.1, f32[64,1024]{1,0:T(8,128)} %bitcast.4, ...), custom_call_target="tpu_custom_call" | custom-call | tf_op jit(solution)/shard_map/pallas_call | solution.py:150
  2.6 25.3 %all_to_all.40.got_ref = bf16[8,16,1920]{2,1,0:T(8,128)(2,1)S(1)} all-to-all(bf16[8,16,1920]{2,1,0:T(8,128)(2,1)S(1)} %get-tuple-element.29), channel_id=1, replica_groups=mesh['dp'=2,'section'=16,'tensor'=8] {'tensor'}, dimensions={0} | all-to-all | bytes 983040 | tf_op jit(solution)/shard_map/all_to_all | solution.py:352
  28.5 12.9 %all_to_all.41.got_ref = bf16[8,16,1024]{2,1,0:T(8,128)(2,1)S(1)} all-to-all(bf16[8,16,1024]{2,1,0:T(8,128)(2,1)S(1)} %shard_map.83), channel_id=1, replica_groups=mesh['dp'=2,'section'=16,'tensor'=8] {'tensor'}, dimensions={0} | all-to-all | bytes 524288 | tf_op jit(solution)/shard_map/all_to_all | solution.py:352
  41.4 0.6 shard_map.84
  42.2 1.6 %collective-permute-start.1 = (s16[16,1152]{1,0:T(8,128)(2,1)S(1)}, s16[16,1152]{1,0:T(8,128)(2,1)S(1)}, u32[]{:S(2)}, u32[]{:S(2)}) collective-permute-start(s16[16,1152]{1,0:T(8,128)(2,1)S(1)} %split.25), channel_id=1, source_target_pairs={{0,8},{8,16},{16,24},{24,32},{32,40},{40,48},{48,56},{56,64},{64,7... | collective-permute-start | bytes 110600 | tf_op jit(solution)/shard_map/ppermute | solution.py:374
  44.3 4.5 %collective-permute-done.1 = s16[16,1152]{1,0:T(8,128)(2,1)S(1)} collective-permute-done((s16[16,1152]{1,0:T(8,128)(2,1)S(1)}, s16[16,1152]{1,0:T(8,128)(2,1)S(1)}, u32[]{:S(2)}, u32[]{:S(2)}) %collective-permute-start.1) | collective-permute-done | bytes 36896 | tf_op jit(solution)/shard_map/ppermute | solution.py:374
  48.8 0.6 shard_map.85
  49.5 13.0 %all_to_all.42.got_ref = bf16[8,16,896]{2,1,0:T(8,128)(2,1)S(1)} all-to-all(bf16[8,16,896]{2,1,0:T(8,128)(2,1)S(1)} %get-tuple-element.37), channel_id=1, replica_groups=mesh['dp'=2,'section'=16,'tensor'=8] {'tensor'}, dimensions={0} | all-to-all | bytes 458752 | tf_op jit(solution)/shard_map/all_to_all | solution.py:352
  63.1 12.9 %all_to_all.43.got_ref = bf16[8,16,1024]{2,1,0:T(8,128)(2,1)S(1)} all-to-all(bf16[8,16,1024]{2,1,0:T(8,128)(2,1)S(1)} %shard_map.86), channel_id=1, replica_groups=mesh['dp'=2,'section'=16,'tensor'=8] {'tensor'}, dimensions={0} | all-to-all | bytes 524288 | tf_op jit(solution)/shard_map/all_to_all | solution.py:352
  76.0 0.6 shard_map.87
  76.7 1.6 %collective-permute-start.4 = (s16[16,1152]{1,0:T(8,128)(2,1)S(1)}, s16[16,1152]{1,0:T(8,128)(2,1)S(1)}, u32[]{:S(2)}, u32[]{:S(2)}) collective-permute-start(s16[16,1152]{1,0:T(8,128)(2,1)S(1)} %split.27), channel_id=1, source_target_pairs={{0,8},{8,16},{16,24},{24,32},{32,40},{40,48},{48,56},{56,64},{64,7... | collective-permute-start | bytes 110600 | tf_op jit(solution)/shard_map/ppermute | solution.py:374
  78.9 4.5 %collective-permute-done.4 = s16[16,1152]{1,0:T(8,128)(2,1)S(1)} collective-permute-done((s16[16,1152]{1,0:T(8,128)(2,1)S(1)}, s16[16,1152]{1,0:T(8,128)(2,1)S(1)}, u32[]{:S(2)}, u32[]{:S(2)}) %collective-permute-start.4) | collective-permute-done | bytes 36896 | tf_op jit(solution)/shard_map/ppermute | solution.py:374
  83.4 0.6 shard_map.88
  84.0 13.0 %all_to_all.44.got_ref = bf16[8,16,896]{2,1,0:T(8,128)(2,1)S(1)} all-to-all(bf16[8,16,896]{2,1,0:T(8,128)(2,1)S(1)} %get-tuple-element.43), channel_id=1, replica_groups=mesh['dp'=2,'section'=16,'tensor'=8] {'tensor'}, dimensions={0} | all-to-all | bytes 458752 | tf_op jit(solution)/shard_map/all_to_all | solution.py:352
  97.6 12.9 %all_to_all.45.got_ref = bf16[8,16,1024]{2,1,0:T(8,128)(2,1)S(1)} all-to-all(bf16[8,16,1024]{2,1,0:T(8,128)(2,1)S(1)} %shard_map.89), channel_id=1, replica_groups=mesh['dp'=2,'section'=16,'tensor'=8] {'tensor'}, dimensions={0} | all-to-all | bytes 524288 | tf_op jit(solution)/shard_map/all_to_all | solution.py:352
  110.5 0.6 shard_map.90
  111.3 1.3 collective-permute-start.7
  113.1 4.8 %collective-permute-done.7 = s16[16,1152]{1,0:T(8,128)(2,1)S(1)} collective-permute-done((s16[16,1152]{1,0:T(8,128)(2,1)S(1)}, s16[16,1152]{1,0:T(8,128)(2,1)S(1)}, u32[]{:S(2)}, u32[]{:S(2)}) %collective-permute-start.7) | collective-permute-done | bytes 36896 | tf_op jit(solution)/shard_map/ppermute | solution.py:374
  117.9 0.6 shard_map.91
  118.6 12.8 %all_to_all.46.got_ref = bf16[8,16,896]{2,1,0:T(8,128)(2,1)S(1)} all-to-all(bf16[8,16,896]{2,1,0:T(8,128)(2,1)S(1)} %get-tuple-element.49), channel_id=1, replica_groups=mesh['dp'=2,'section'=16,'tensor'=8] {'tensor'}, dimensions={0} | all-to-all | bytes 458752 | tf_op jit(solution)/shard_map/all_to_all | solution.py:352
  132.0 11.5 %all_to_all.47.got_ref = bf16[8,16,512]{2,1,0:T(8,128)(2,1)S(1)} all-to-all(bf16[8,16,512]{2,1,0:T(8,128)(2,1)S(1)} %shard_map.92), channel_id=1, replica_groups=mesh['dp'=2,'section'=16,'tensor'=8] {'tensor'}, dimensions={0} | all-to-all | bytes 262144 | tf_op jit(solution)/shard_map/all_to_all | solution.py:352
  144.2 1.2 collective-permute-start.10
  145.4 5.4 %collective-permute-done.10 = s16[16,1152]{1,0:T(8,128)(2,1)S(1)} collective-permute-done((s16[16,1152]{1,0:T(8,128)(2,1)S(1)}, s16[16,1152]{1,0:T(8,128)(2,1)S(1)}, u32[]{:S(2)}, u32[]{:S(2)}) %collective-permute-start.10) | collective-permute-done | bytes 36896 | tf_op jit(solution)/shard_map/ppermute | solution.py:374
  150.8 0.8 shard_map.94
  (35 shorter events, 5.0 us)
Async XLA Ops:
  0.0 41.4 %copy-start.1 = (bf16[1,2,1024,1024]{3,2,1,0:T(8,128)(2,1)S(1)}, bf16[1,2,1024,1024]{3,2,1,0:T(8,128)(2,1)}, u32[]{:S(2)}) copy-start(bf16[1,2,1024,1024]{3,2,1,0:T(8,128)(2,1)} %weight_ref.7) | copy-start | bytes 12582916
  2.6 46.2 %copy-start = (bf16[1,2,1024,1280]{3,2,1,0:T(8,128)(2,1)S(1)}, bf16[1,2,1024,1280]{3,2,1,0:T(8,128)(2,1)}, u32[]{:S(2)}) copy-start(bf16[1,2,1024,1280]{3,2,1,0:T(8,128)(2,1)} %refs_2_.5) | copy-start | bytes 15728644
  42.1 6.8 %collective-permute-start = (s16[48,1152]{1,0:T(8,128)(2,1)S(1)}, s16[48,1152]{1,0:T(8,128)(2,1)S(1)}, u32[]{:S(2)}, u32[]{:S(2)}) collective-permute-start(s16[48,1152]{1,0:T(8,128)(2,1)S(1)} %split.24), channel_id=1, source_target_pairs={{0,8},{8,16},{16,24},{24,32},{32,40},{40,48},{48,56},{56,64},{64,7... | collective-permute-start | bytes 331784 | tf_op jit(solution)/shard_map/ppermute | solution.py:374
  42.2 6.7 %collective-permute-start.1 = (s16[16,1152]{1,0:T(8,128)(2,1)S(1)}, s16[16,1152]{1,0:T(8,128)(2,1)S(1)}, u32[]{:S(2)}, u32[]{:S(2)}) collective-permute-start(s16[16,1152]{1,0:T(8,128)(2,1)S(1)} %split.25), channel_id=1, source_target_pairs={{0,8},{8,16},{16,24},{24,32},{32,40},{40,48},{48,56},{56,64},{64,7... | collective-permute-start | bytes 110600 | tf_op jit(solution)/shard_map/ppermute | solution.py:374
  43.7 5.8 %collective-permute-start.2 = (bf16[8,16,512]{2,1,0:T(8,128)(2,1)S(1)}, bf16[8,16,512]{2,1,0:T(8,128)(2,1)S(1)}, u32[]{:S(2)}, u32[]{:S(2)}) collective-permute-start(bf16[8,16,512]{2,1,0:T(8,128)(2,1)S(1)} %get-tuple-element.36.refs_0_), channel_id=1, source_target_pairs={{0,1},{1,0},{2,3},{3,2},{4,5},{5,4},{6,7},{7,6},{8,9},{9,8},{10,11... | collective-permute-start | bytes 393224 | tf_op jit(solution)/shard_map/ppermute | solution.py:378
  76.6 6.8 %collective-permute-start.3 = (s16[48,1152]{1,0:T(8,128)(2,1)S(1)}, s16[48,1152]{1,0:T(8,128)(2,1)S(1)}, u32[]{:S(2)}, u32[]{:S(2)}) collective-permute-start(s16[48,1152]{1,0:T(8,128)(2,1)S(1)} %split.26), channel_id=1, source_target_pairs={{0,8},{8,16},{16,24},{24,32},{32,40},{40,48},{48,56},{56,64},{64,7... | collective-permute-start | bytes 331784 | tf_op jit(solution)/shard_map/ppermute | solution.py:374
  76.7 6.7 %collective-permute-start.4 = (s16[16,1152]{1,0:T(8,128)(2,1)S(1)}, s16[16,1152]{1,0:T(8,128)(2,1)S(1)}, u32[]{:S(2)}, u32[]{:S(2)}) collective-permute-start(s16[16,1152]{1,0:T(8,128)(2,1)S(1)} %split.27), channel_id=1, source_target_pairs={{0,8},{8,16},{16,24},{24,32},{32,40},{40,48},{48,56},{56,64},{64,7... | collective-permute-start | bytes 110600 | tf_op jit(solution)/shard_map/ppermute | solution.py:374
  78.3 5.7 %collective-permute-start.5 = (bf16[8,16,512]{2,1,0:T(8,128)(2,1)S(1)}, bf16[8,16,512]{2,1,0:T(8,128)(2,1)S(1)}, u32[]{:S(2)}, u32[]{:S(2)}) collective-permute-start(bf16[8,16,512]{2,1,0:T(8,128)(2,1)S(1)} %get-tuple-element.42.refs_0_), channel_id=1, source_target_pairs={{0,1},{1,0},{2,3},{3,2},{4,5},{5,4},{6,7},{7,6},{8,9},{9,8},{10,11... | collective-permute-start | bytes 393224 | tf_op jit(solution)/shard_map/ppermute | solution.py:378
  111.2 6.8 %collective-permute-start.6 = (s16[48,1152]{1,0:T(8,128)(2,1)S(1)}, s16[48,1152]{1,0:T(8,128)(2,1)S(1)}, u32[]{:S(2)}, u32[]{:S(2)}) collective-permute-start(s16[48,1152]{1,0:T(8,128)(2,1)S(1)} %split.28), channel_id=1, source_target_pairs={{0,8},{8,16},{16,24},{24,32},{32,40},{40,48},{48,56},{56,64},{64,7... | collective-permute-start | bytes 331784 | tf_op jit(solution)/shard_map/ppermute | solution.py:374
  111.3 6.7 %collective-permute-start.7 = (s16[16,1152]{1,0:T(8,128)(2,1)S(1)}, s16[16,1152]{1,0:T(8,128)(2,1)S(1)}, u32[]{:S(2)}, u32[]{:S(2)}) collective-permute-start(s16[16,1152]{1,0:T(8,128)(2,1)S(1)} %split.29), channel_id=1, source_target_pairs={{0,8},{8,16},{16,24},{24,32},{32,40},{40,48},{48,56},{56,64},{64,7... | collective-permute-start | bytes 110600 | tf_op jit(solution)/shard_map/ppermute | solution.py:374
  112.6 6.0 %collective-permute-start.8 = (bf16[8,16,512]{2,1,0:T(8,128)(2,1)S(1)}, bf16[8,16,512]{2,1,0:T(8,128)(2,1)S(1)}, u32[]{:S(2)}, u32[]{:S(2)}) collective-permute-start(bf16[8,16,512]{2,1,0:T(8,128)(2,1)S(1)} %get-tuple-element.48.refs_0_), channel_id=1, source_target_pairs={{0,1},{1,0},{2,3},{3,2},{4,5},{5,4},{6,7},{7,6},{8,9},{9,8},{10,11... | collective-permute-start | bytes 393224 | tf_op jit(solution)/shard_map/ppermute | solution.py:378
  144.1 6.8 %collective-permute-start.9 = (s16[48,1152]{1,0:T(8,128)(2,1)S(1)}, s16[48,1152]{1,0:T(8,128)(2,1)S(1)}, u32[]{:S(2)}, u32[]{:S(2)}) collective-permute-start(s16[48,1152]{1,0:T(8,128)(2,1)S(1)} %split.32), channel_id=1, source_target_pairs={{0,8},{8,16},{16,24},{24,32},{32,40},{40,48},{48,56},{56,64},{64,7... | collective-permute-start | bytes 331784 | tf_op jit(solution)/shard_map/ppermute | solution.py:374
  144.2 6.7 %collective-permute-start.10 = (s16[16,1152]{1,0:T(8,128)(2,1)S(1)}, s16[16,1152]{1,0:T(8,128)(2,1)S(1)}, u32[]{:S(2)}, u32[]{:S(2)}) collective-permute-start(s16[16,1152]{1,0:T(8,128)(2,1)S(1)} %split.33), channel_id=1, source_target_pairs={{0,8},{8,16},{16,24},{24,32},{32,40},{40,48},{48,56},{56,64},{64,7... | collective-permute-start | bytes 110600 | tf_op jit(solution)/shard_map/ppermute | solution.py:374

commit v6 on v5

--- a/solution.py
+++ b/solution.py
@@ -23,7 +23,6 @@
 PIECE = 896
 CHUNKS = 8
 TOP = 125.0
-PARTS = 1
 VMEM_LIMIT = 16 * 1024 * 1024
 
 VMEM = pl.BlockSpec(memory_space=pltpu.VMEM)
@@ -175,42 +174,51 @@
     return jnp.exp2(power) / jnp.where(power < TOP, 32767.0, 4095.0)
 
 
-def pack(packed_ref, state):
+def pack(early_ref, late_ref, state):
     width = state.shape[1]
     peak = jnp.max(jnp.abs(state), axis=-1, keepdims=True)
     power = jnp.clip(jnp.ceil(jnp.log2(jnp.maximum(peak, 1e-37))), -TOP, TOP)
     ratio = state * jnp.exp2(-power) * jnp.where(power < TOP, 32767.0, 4095.0)
-    steps = jnp.clip(jnp.round(ratio), -32767.0, 32767.0)
-    packed_ref[:, :width] = steps.astype(jnp.int32).astype(jnp.int16)
-    powers = jnp.broadcast_to(power.astype(jnp.int32), (state.shape[0], HEAD))
-    packed_ref[:, width:] = powers.astype(jnp.int16)
-
-
-def unpack(packed_ref):
-    width = packed_ref.shape[1] - HEAD
-    power = packed_ref[:, width:].astype(jnp.int32).astype(f32)[:, :1]
-    return packed_ref[:, :width].astype(jnp.int32).astype(f32) * unit_of(power)
-
-
-def expand_kernel(*refs):
-    *packed_refs, out_ref = refs
-    out_ref[...] = jnp.concatenate([unpack(packed_ref) for packed_ref in packed_refs], axis=0)
+    steps = jnp.clip(jnp.round(ratio), -32767.0, 32767.0).astype(jnp.int32).astype(jnp.int16)
+    rows = early_ref.shape[0]
+    early_ref[...] = steps[:rows]
+    late_ref[:, :width] = steps[rows:]
+    slots = state.shape[0] // TREE
+    lane = lax.broadcasted_iota(jnp.int32, (TREE, HEAD), 1)
+    powers = jnp.zeros((TREE, HEAD), f32)
+    for slot in range(slots):
+        mine = power[slot * TREE : (slot + 1) * TREE]
+        powers = jnp.where(lane >= slot * (HEAD // slots), mine, powers)
+    late_ref[:, width:] = powers.astype(jnp.int32).astype(jnp.int16)
+
+
+def unpack(steps_ref, powers_ref):
+    slots = steps_ref.shape[0] // TREE
+    powers = powers_ref[...].astype(jnp.int32).astype(f32)
+    gap = HEAD // slots
+    power = jnp.concatenate(
+        [powers[:, slot * gap : slot * gap + 1] for slot in range(slots)], axis=0
+    )
+    return steps_ref[...].astype(jnp.int32).astype(f32) * unit_of(power)
+
+
+def expand_kernel(steps_ref, powers_ref, out_ref):
+    out_ref[...] = unpack(steps_ref, powers_ref)
 
 
 def expand(packed):
-    rows, width = packed[0].shape
     return pl.pallas_call(
         expand_kernel,
-        out_shape=jax.ShapeDtypeStruct((rows * len(packed), width - HEAD), f32),
-        in_specs=[VMEM] * len(packed),
+        out_shape=jax.ShapeDtypeStruct(packed[0].shape, f32),
+        in_specs=[VMEM] * 2,
         out_specs=VMEM,
         compiler_params=PARAMS,
     )(*packed)
 
 
 def project_kernel(*refs, step):
-    *packed_refs, gain_ref, weight_ref, out_ref, state_ref = refs
-    state = jnp.concatenate([unpack(packed_ref) for packed_ref in packed_refs], axis=0)
+    steps_ref, powers_ref, gain_ref, weight_ref, out_ref, state_ref = refs
+    state = unpack(steps_ref, powers_ref)
     state_ref[...] = state
     which = layer_of(step)
     scaled = (state * gain_ref[pl.ds(which, 1), :]).astype(bf16)
@@ -220,12 +228,11 @@
 
 def project(packed, gain, weight, step):
     rows, width = packed[0].shape
-    rows *= len(packed)
     return pl.pallas_call(
         functools.partial(project_kernel, step=step),
         out_shape=(
             jax.ShapeDtypeStruct((2 * rows // TREE, TREE, PIECE), bf16),
-            jax.ShapeDtypeStruct((rows, width - HEAD), f32),
+            jax.ShapeDtypeStruct((rows, width), f32),
         ),
         in_specs=[VMEM] * (2 + len(packed)),
         out_specs=(VMEM,) * 2,
@@ -326,16 +333,16 @@
     )
 
     delta = jnp.dot(attended, weight_ref[0, layer_of(step)], preferred_element_type=f32)
-    state = state_ref[...] + delta
-    rows = out_refs[0].shape[0]
-    for part, out_ref in enumerate(out_refs):
-        pack(out_ref, state[part * rows : (part + 1) * rows])
+    pack(*out_refs, state_ref[...] + delta)
 
 
 def update(state, got, weight, step):
     rows, width = state.shape
     count, tree, total = got.shape
-    out_shape = (jax.ShapeDtypeStruct((rows // PARTS, width + HEAD), jnp.int16),) * PARTS
+    out_shape = (
+        jax.ShapeDtypeStruct((rows - TREE, width), jnp.int16),
+        jax.ShapeDtypeStruct((TREE, width + HEAD), jnp.int16),
+    )
     last = total == HALF
     if not last:
         out_shape += (jax.ShapeDtypeStruct((count, tree, total - HALF), bf16),)
@@ -371,10 +378,11 @@
         else:
             spread = attend(exchange(pieces), table, cache, step)
         outs = update(state, exchange(spread), w_out, step)
-        parts = [lax.ppermute(part, "section", ring) for part in jnp.split(outs[0], [48])]
-        packed = [jnp.concatenate(parts)]
-        if len(outs) > 1:
-            mine = outs[1]
+        early, late = (lax.ppermute(part, "section", ring) for part in outs[:2])
+        width = early.shape[1]
+        packed = (jnp.concatenate([early, late[:, :width]]), late[:, width:])
+        if len(outs) > 2:
+            mine = outs[2]
             come = lax.ppermute(mine, "tensor", mates)
     return expand(packed).reshape(hidden_in.shape)
 

time: 152 us -> 152 us (level)
  no operation moved by 1% of the time
where the time goes in v6:
time: 152 us; the launch traced here: 151 us
  blocking collectives  114 us (75%)
  waiting for transfers between devices  18.7 us (12%)
  Pallas kernels  10.2 us (7%)
  starting transfers between devices  7.78 us (5%)
    all_to_all x8, blocking collectives, exchange(): return lax.all_to_all(value, 'tensor', 0, 0, tiled=True)  114 us
    ppermute x8, waiting for transfers between devices, body(): early, late = (lax.ppermute(part, 'section', ring) for part in outs[:2])  18.7 us
    ppermute x8, starting transfers between devices, body(): early, late = (lax.ppermute(part, 'section', ring) for part in outs[:2])  6.08 us
  transfers between devices with their start and end apart: 11, of which 4 were waited for; matrix products, arithmetic and copies ran while one was open for 0% of the time, Pallas kernels for 1%

profile of v6, /device:TPU:16, one launch (start us, length us, event | category | flops | bytes accessed | tf_op | source)
XLA Modules:
  0.0 151.4 jit_solution(18102396577267627572)
XLA Ops:
  0.0 2.6 %shard_map.82 = (bf16[8,16,1920]{2,1,0:T(8,128)(2,1)S(1)}, f32[64,1024]{1,0:T(8,128)S(1)}, f32[4,16,128]{2,1,0:T(8,128)S(1)}, f32[2,1024]{1,0:T(2,128)S(1)}, bf16[4,4,64,256]{3,2,1,0:T(8,128)(2,1)S(1)}) custom-call(s32[4,16]{1,0:T(4,128)} %bitcast.8, s32[16,64]{1,0:T(8,128)} %bitcast.7, s32[64]{0:T(128)} %lengths_far.1, f32[64,1024]{1,0:T(8,128)} %bitcast.6, ...), custom_call_target="tpu_custom_call" | custom-call | tf_op jit(solution)/shard_map/pallas_call | solution.py:149
  2.6 25.3 %all_to_all.40.got_ref = bf16[8,16,1920]{2,1,0:T(8,128)(2,1)S(1)} all-to-all(bf16[8,16,1920]{2,1,0:T(8,128)(2,1)S(1)} %get-tuple-element.34), channel_id=1, replica_groups=mesh['dp'=2,'section'=16,'tensor'=8] {'tensor'}, dimensions={0} | all-to-all | bytes 983040 | tf_op jit(solution)/shard_map/all_to_all | solution.py:359
  28.5 12.9 %all_to_all.41.got_ref = bf16[8,16,1024]{2,1,0:T(8,128)(2,1)S(1)} all-to-all(bf16[8,16,1024]{2,1,0:T(8,128)(2,1)S(1)} %shard_map.83), channel_id=1, replica_groups=mesh['dp'=2,'section'=16,'tensor'=8] {'tensor'}, dimensions={0} | all-to-all | bytes 524288 | tf_op jit(solution)/shard_map/all_to_all | solution.py:359
  42.1 1.6 %collective-permute-start.1 = (s16[16,1152]{1,0:T(8,128)(2,1)S(1)}, s16[16,1152]{1,0:T(8,128)(2,1)S(1)}, u32[]{:S(2)}, u32[]{:S(2)}) collective-permute-start(s16[16,1152]{1,0:T(8,128)(2,1)S(1)} %get-tuple-element.38), channel_id=1, source_target_pairs={{0,8},{8,16},{16,24},{24,32},{32,40},{40,48},{48,56},{56,64},{64,7... | collective-permute-start | bytes 110600 | tf_op jit(solution)/shard_map/ppermute | solution.py:381
  44.3 4.4 %collective-permute-done.1 = s16[16,1152]{1,0:T(8,128)(2,1)S(1)} collective-permute-done((s16[16,1152]{1,0:T(8,128)(2,1)S(1)}, s16[16,1152]{1,0:T(8,128)(2,1)S(1)}, u32[]{:S(2)}, u32[]{:S(2)}) %collective-permute-start.1) | collective-permute-done | bytes 36896 | tf_op jit(solution)/shard_map/ppermute | solution.py:381
  48.7 0.7 shard_map.85
  49.4 13.1 %all_to_all.42.got_ref = bf16[8,16,896]{2,1,0:T(8,128)(2,1)S(1)} all-to-all(bf16[8,16,896]{2,1,0:T(8,128)(2,1)S(1)} %get-tuple-element.43), channel_id=1, replica_groups=mesh['dp'=2,'section'=16,'tensor'=8] {'tensor'}, dimensions={0} | all-to-all | bytes 458752 | tf_op jit(solution)/shard_map/all_to_all | solution.py:359
  63.0 12.9 %all_to_all.43.got_ref = bf16[8,16,1024]{2,1,0:T(8,128)(2,1)S(1)} all-to-all(bf16[8,16,1024]{2,1,0:T(8,128)(2,1)S(1)} %shard_map.86), channel_id=1, replica_groups=mesh['dp'=2,'section'=16,'tensor'=8] {'tensor'}, dimensions={0} | all-to-all | bytes 524288 | tf_op jit(solution)/shard_map/all_to_all | solution.py:359
  75.9 0.6 shard_map.87
  76.6 1.6 %collective-permute-start.4 = (s16[16,1152]{1,0:T(8,128)(2,1)S(1)}, s16[16,1152]{1,0:T(8,128)(2,1)S(1)}, u32[]{:S(2)}, u32[]{:S(2)}) collective-permute-start(s16[16,1152]{1,0:T(8,128)(2,1)S(1)} %get-tuple-element.46), channel_id=1, source_target_pairs={{0,8},{8,16},{16,24},{24,32},{32,40},{40,48},{48,56},{56,64},{64,7... | collective-permute-start | bytes 110600 | tf_op jit(solution)/shard_map/ppermute | solution.py:381
  78.8 4.4 %collective-permute-done.4 = s16[16,1152]{1,0:T(8,128)(2,1)S(1)} collective-permute-done((s16[16,1152]{1,0:T(8,128)(2,1)S(1)}, s16[16,1152]{1,0:T(8,128)(2,1)S(1)}, u32[]{:S(2)}, u32[]{:S(2)}) %collective-permute-start.4) | collective-permute-done | bytes 36896 | tf_op jit(solution)/shard_map/ppermute | solution.py:381
  83.2 0.7 shard_map.88
  83.9 13.1 %all_to_all.44.got_ref = bf16[8,16,896]{2,1,0:T(8,128)(2,1)S(1)} all-to-all(bf16[8,16,896]{2,1,0:T(8,128)(2,1)S(1)} %get-tuple-element.50), channel_id=1, replica_groups=mesh['dp'=2,'section'=16,'tensor'=8] {'tensor'}, dimensions={0} | all-to-all | bytes 458752 | tf_op jit(solution)/shard_map/all_to_all | solution.py:359
  97.6 12.9 %all_to_all.45.got_ref = bf16[8,16,1024]{2,1,0:T(8,128)(2,1)S(1)} all-to-all(bf16[8,16,1024]{2,1,0:T(8,128)(2,1)S(1)} %shard_map.89), channel_id=1, replica_groups=mesh['dp'=2,'section'=16,'tensor'=8] {'tensor'}, dimensions={0} | all-to-all | bytes 524288 | tf_op jit(solution)/shard_map/all_to_all | solution.py:359
  110.4 0.6 shard_map.90
  111.2 1.3 collective-permute-start.7
  113.0 4.7 %collective-permute-done.7 = s16[16,1152]{1,0:T(8,128)(2,1)S(1)} collective-permute-done((s16[16,1152]{1,0:T(8,128)(2,1)S(1)}, s16[16,1152]{1,0:T(8,128)(2,1)S(1)}, u32[]{:S(2)}, u32[]{:S(2)}) %collective-permute-start.7) | collective-permute-done | bytes 36896 | tf_op jit(solution)/shard_map/ppermute | solution.py:381
  117.7 0.7 shard_map.91
  118.4 12.8 %all_to_all.46.got_ref = bf16[8,16,896]{2,1,0:T(8,128)(2,1)S(1)} all-to-all(bf16[8,16,896]{2,1,0:T(8,128)(2,1)S(1)} %get-tuple-element.57), channel_id=1, replica_groups=mesh['dp'=2,'section'=16,'tensor'=8] {'tensor'}, dimensions={0} | all-to-all | bytes 458752 | tf_op jit(solution)/shard_map/all_to_all | solution.py:359
  131.8 11.5 %all_to_all.47.got_ref = bf16[8,16,512]{2,1,0:T(8,128)(2,1)S(1)} all-to-all(bf16[8,16,512]{2,1,0:T(8,128)(2,1)S(1)} %shard_map.92), channel_id=1, replica_groups=mesh['dp'=2,'section'=16,'tensor'=8] {'tensor'}, dimensions={0} | all-to-all | bytes 262144 | tf_op jit(solution)/shard_map/all_to_all | solution.py:359
  143.3 0.6 shard_map.93
  144.0 1.3 collective-permute-start.10
  145.3 5.3 %collective-permute-done.10 = s16[16,1152]{1,0:T(8,128)(2,1)S(1)} collective-permute-done((s16[16,1152]{1,0:T(8,128)(2,1)S(1)}, s16[16,1152]{1,0:T(8,128)(2,1)S(1)}, u32[]{:S(2)}, u32[]{:S(2)}) %collective-permute-start.10) | collective-permute-done | bytes 36896 | tf_op jit(solution)/shard_map/ppermute | solution.py:381
  150.6 0.9 shard_map.94
  (38 shorter events, 5.0 us)
Async XLA Ops:
  0.0 41.4 %copy-start = (bf16[1,2,1024,1024]{3,2,1,0:T(8,128)(2,1)S(1)}, bf16[1,2,1024,1024]{3,2,1,0:T(8,128)(2,1)}, u32[]{:S(2)}) copy-start(bf16[1,2,1024,1024]{3,2,1,0:T(8,128)(2,1)} %weight_ref.7) | copy-start | bytes 12582916
  0.0 48.7 %slice-start = ((s8[5242880]{0:T(1024)(128)(4,1)}), s8[4194304]{0:T(1024)(128)(4,1)S(1)}, s32[]{:S(2)}) async-start(s8[5242880]{0:T(1024)(128)(4,1)} %bitcast.4), calls=%async_computation.8 | async-start | bytes 8388608
  2.6 46.1 %slice-start.1 = ((s8[5242880]{0:T(1024)(128)(4,1)}), s8[1048576]{0:T(1024)(128)(4,1)S(1)}, s32[]{:S(2)}) async-start(s8[5242880]{0:T(1024)(128)(4,1)} %bitcast.4), calls=%async_computation.9 | async-start | bytes 2097152
  42.0 6.6 %collective-permute-start = (s16[48,1024]{1,0:T(8,128)(2,1)S(1)}, s16[48,1024]{1,0:T(8,128)(2,1)S(1)}, u32[]{:S(2)}, u32[]{:S(2)}) collective-permute-start(s16[48,1024]{1,0:T(8,128)(2,1)S(1)} %get-tuple-element.37), channel_id=1, source_target_pairs={{0,8},{8,16},{16,24},{24,32},{32,40},{40,48},{48,56},{56,64},{64,7... | collective-permute-start | bytes 294920 | tf_op jit(solution)/shard_map/ppermute | solution.py:381
  42.1 6.5 %collective-permute-start.1 = (s16[16,1152]{1,0:T(8,128)(2,1)S(1)}, s16[16,1152]{1,0:T(8,128)(2,1)S(1)}, u32[]{:S(2)}, u32[]{:S(2)}) collective-permute-start(s16[16,1152]{1,0:T(8,128)(2,1)S(1)} %get-tuple-element.38), channel_id=1, source_target_pairs={{0,8},{8,16},{16,24},{24,32},{32,40},{40,48},{48,56},{56,64},{64,7... | collective-permute-start | bytes 110600 | tf_op jit(solution)/shard_map/ppermute | solution.py:381
  43.7 5.7 %collective-permute-start.2 = (bf16[8,16,512]{2,1,0:T(8,128)(2,1)S(1)}, bf16[8,16,512]{2,1,0:T(8,128)(2,1)S(1)}, u32[]{:S(2)}, u32[]{:S(2)}) collective-permute-start(bf16[8,16,512]{2,1,0:T(8,128)(2,1)S(1)} %get-tuple-element.42.refs_0_), channel_id=1, source_target_pairs={{0,1},{1,0},{2,3},{3,2},{4,5},{5,4},{6,7},{7,6},{8,9},{9,8},{10,11... | collective-permute-start | bytes 393224 | tf_op jit(solution)/shard_map/ppermute | solution.py:386
  76.6 6.6 %collective-permute-start.3 = (s16[48,1024]{1,0:T(8,128)(2,1)S(1)}, s16[48,1024]{1,0:T(8,128)(2,1)S(1)}, u32[]{:S(2)}, u32[]{:S(2)}) collective-permute-start(s16[48,1024]{1,0:T(8,128)(2,1)S(1)} %get-tuple-element.45), channel_id=1, source_target_pairs={{0,8},{8,16},{16,24},{24,32},{32,40},{40,48},{48,56},{56,64},{64,7... | collective-permute-start | bytes 294920 | tf_op jit(solution)/shard_map/ppermute | solution.py:381
  76.6 6.5 %collective-permute-start.4 = (s16[16,1152]{1,0:T(8,128)(2,1)S(1)}, s16[16,1152]{1,0:T(8,128)(2,1)S(1)}, u32[]{:S(2)}, u32[]{:S(2)}) collective-permute-start(s16[16,1152]{1,0:T(8,128)(2,1)S(1)} %get-tuple-element.46), channel_id=1, source_target_pairs={{0,8},{8,16},{16,24},{24,32},{32,40},{40,48},{48,56},{56,64},{64,7... | collective-permute-start | bytes 110600 | tf_op jit(solution)/shard_map/ppermute | solution.py:381
  78.2 5.7 %collective-permute-start.5 = (bf16[8,16,512]{2,1,0:T(8,128)(2,1)S(1)}, bf16[8,16,512]{2,1,0:T(8,128)(2,1)S(1)}, u32[]{:S(2)}, u32[]{:S(2)}) collective-permute-start(bf16[8,16,512]{2,1,0:T(8,128)(2,1)S(1)} %get-tuple-element.49.refs_0_), channel_id=1, source_target_pairs={{0,1},{1,0},{2,3},{3,2},{4,5},{5,4},{6,7},{7,6},{8,9},{9,8},{10,11... | collective-permute-start | bytes 393224 | tf_op jit(solution)/shard_map/ppermute | solution.py:386
  111.1 6.6 %collective-permute-start.6 = (s16[48,1024]{1,0:T(8,128)(2,1)S(1)}, s16[48,1024]{1,0:T(8,128)(2,1)S(1)}, u32[]{:S(2)}, u32[]{:S(2)}) collective-permute-start(s16[48,1024]{1,0:T(8,128)(2,1)S(1)} %get-tuple-element.52), channel_id=1, source_target_pairs={{0,8},{8,16},{16,24},{24,32},{32,40},{40,48},{48,56},{56,64},{64,7... | collective-permute-start | bytes 294920 | tf_op jit(solution)/shard_map/ppermute | solution.py:381
  111.2 6.5 %collective-permute-start.7 = (s16[16,1152]{1,0:T(8,128)(2,1)S(1)}, s16[16,1152]{1,0:T(8,128)(2,1)S(1)}, u32[]{:S(2)}, u32[]{:S(2)}) collective-permute-start(s16[16,1152]{1,0:T(8,128)(2,1)S(1)} %get-tuple-element.53), channel_id=1, source_target_pairs={{0,8},{8,16},{16,24},{24,32},{32,40},{40,48},{48,56},{56,64},{64,7... | collective-permute-start | bytes 110600 | tf_op jit(solution)/shard_map/ppermute | solution.py:381
  112.5 5.9 %collective-permute-start.8 = (bf16[8,16,512]{2,1,0:T(8,128)(2,1)S(1)}, bf16[8,16,512]{2,1,0:T(8,128)(2,1)S(1)}, u32[]{:S(2)}, u32[]{:S(2)}) collective-permute-start(bf16[8,16,512]{2,1,0:T(8,128)(2,1)S(1)} %get-tuple-element.56.refs_0_), channel_id=1, source_target_pairs={{0,1},{1,0},{2,3},{3,2},{4,5},{5,4},{6,7},{7,6},{8,9},{9,8},{10,11... | collective-permute-start | bytes 393224 | tf_op jit(solution)/shard_map/ppermute | solution.py:386
  143.9 6.6 %collective-permute-start.9 = (s16[48,1024]{1,0:T(8,128)(2,1)S(1)}, s16[48,1024]{1,0:T(8,128)(2,1)S(1)}, u32[]{:S(2)}, u32[]{:S(2)}) collective-permute-start(s16[48,1024]{1,0:T(8,128)(2,1)S(1)} %get-tuple-element.59), channel_id=1, source_target_pairs={{0,8},{8,16},{16,24},{24,32},{32,40},{40,48},{48,56},{56,64},{64,7... | collective-permute-start | bytes 294920 | tf_op jit(solution)/shard_map/ppermute | solution.py:381
  144.0 6.5 %collective-permute-start.10 = (s16[16,1152]{1,0:T(8,128)(2,1)S(1)}, s16[16,1152]{1,0:T(8,128)(2,1)S(1)}, u32[]{:S(2)}, u32[]{:S(2)}) collective-permute-start(s16[16,1152]{1,0:T(8,128)(2,1)S(1)} %get-tuple-element.60), channel_id=1, source_target_pairs={{0,8},{8,16},{16,24},{24,32},{32,40},{40,48},{48,56},{56,64},{64,7... | collective-permute-start | bytes 110600 | tf_op jit(solution)/shard_map/ppermute | solution.py:381

commit v7 on v6

--- a/solution.py
+++ b/solution.py
@@ -21,7 +21,7 @@
 HALF = 512
 MIX = 768
 PIECE = 896
-CHUNKS = 8
+CHUNKS = 4
 TOP = 125.0
 VMEM_LIMIT = 16 * 1024 * 1024
 
@@ -88,8 +88,8 @@
 
 def first_kernel(
     assign_far, parents_far, lengths_far, state_far, gain_far, weight_far, cache_far,
-    out_ref, state_ref, table_ref, gain_ref, cache_ref,
-    assign_ref, parents_ref, lengths_ref, rows, weight_ref, sems, more,
+    out_ref, state_ref, table_ref, gain_ref,
+    assign_ref, parents_ref, lengths_ref, rows, weight_ref, cache_ref, sems, more,
 ):
     weight_copies = loads(weight_far.at[0, 0], weight_ref, sems)
     other = [
@@ -101,7 +101,7 @@
                 (lengths_far, lengths_ref),
                 (state_far, state_ref),
                 (gain_far.at[0], gain_ref),
-                (cache_far.at[0], cache_ref),
+                (cache_far.at[0, pl.ds(0, 1)], cache_ref),
             )
         )
     ]
@@ -153,16 +153,16 @@
             pltpu.VMEM((slots * tree, width), f32),
             pltpu.VMEM((steps, TREE, HEAD), f32),
             pltpu.VMEM(gain.shape[1:], f32),
-            pltpu.VMEM(cache.shape[1:], bf16),
         ),
         in_specs=[FAR] * 7,
-        out_specs=(VMEM,) * 5,
+        out_specs=(VMEM,) * 4,
         scratch_shapes=[
             pltpu.SMEM(assign.shape[::-1], jnp.int32),
             pltpu.SMEM(parents.shape[::-1], jnp.int32),
             pltpu.SMEM(lengths.shape, jnp.int32),
             pltpu.VMEM((steps, TREE, HEAD), f32),
             pltpu.VMEM(weight.shape[2:], bf16),
+            pltpu.VMEM((1,) + cache.shape[2:], bf16),
             pltpu.SemaphoreType.DMA((CHUNKS,)),
             pltpu.SemaphoreType.DMA((6,)),
         ],
@@ -366,7 +366,8 @@
 def body(hidden_in, norm_gain, w_qkv, w_out, kv_cache, parents, lengths, assign):
     sections = lax.axis_size("section")
     ring = [(s, (s + 1) % sections) for s in range(sections)]
-    pieces, state, table, gain, cache = first(
+    cache = kv_cache.reshape(kv_cache.shape[1:])
+    pieces, state, table, gain = first(
         assign, parents, lengths, hidden_in, norm_gain, w_qkv, kv_cache
     )
     mates = [(t, t ^ 1) for t in range(pieces.shape[0])]

time: 152 us -> 151 us (level)
  no operation moved by 1% of the time
where the time goes in v7:
time: 151 us
  blocking collectives  114 us (75%)
  waiting for transfers between devices  18.7 us (12%)
  Pallas kernels  9.92 us (7%)
  starting transfers between devices  7.78 us (5%)
    all_to_all x8, blocking collectives, exchange(): return lax.all_to_all(value, 'tensor', 0, 0, tiled=True)  114 us
    ppermute x8, waiting for transfers between devices, body(): early, late = (lax.ppermute(part, 'section', ring) for part in outs[:2])  18.7 us
    ppermute x8, starting transfers between devices, body(): early, late = (lax.ppermute(part, 'section', ring) for part in outs[:2])  6.08 us
  transfers between devices with their start and end apart: 11, of which 4 were waited for; matrix products, arithmetic and copies ran while one was open for 0% of the time, Pallas kernels for 1%

profile of v7, /device:TPU:16, one launch (start us, length us, event | category | flops | bytes accessed | tf_op | source)
XLA Modules:
  0.0 151.1 jit_solution(13570549136542461889)
XLA Ops:
  0.0 2.3 %shard_map.82 = (bf16[8,16,1920]{2,1,0:T(8,128)(2,1)S(1)}, f32[64,1024]{1,0:T(8,128)S(1)}, f32[4,16,128]{2,1,0:T(8,128)S(1)}, f32[2,1024]{1,0:T(2,128)S(1)}) custom-call(s32[4,16]{1,0:T(4,128)} %bitcast.13, s32[16,64]{1,0:T(8,128)} %bitcast.12, s32[64]{0:T(128)} %lengths_far.1, f32[64,1024]{1,0:T(8,128)} %bitcast.11, f32[1,2,1024]{2,1,0:T(2,128)} %gain_far.1, ...), custom_call_target="tpu_custom_call" | custom-call | tf_op jit(solution)/shard_map/pallas_call | solution.py:149
  2.3 25.3 %all_to_all.40.got_ref = bf16[8,16,1920]{2,1,0:T(8,128)(2,1)S(1)} all-to-all(bf16[8,16,1920]{2,1,0:T(8,128)(2,1)S(1)} %get-tuple-element.33), channel_id=1, replica_groups=mesh['dp'=2,'section'=16,'tensor'=8] {'tensor'}, dimensions={0} | all-to-all | bytes 983040 | tf_op jit(solution)/shard_map/all_to_all | solution.py:359
  28.2 12.9 %all_to_all.41.got_ref = bf16[8,16,1024]{2,1,0:T(8,128)(2,1)S(1)} all-to-all(bf16[8,16,1024]{2,1,0:T(8,128)(2,1)S(1)} %shard_map.83), channel_id=1, replica_groups=mesh['dp'=2,'section'=16,'tensor'=8] {'tensor'}, dimensions={0} | all-to-all | bytes 524288 | tf_op jit(solution)/shard_map/all_to_all | solution.py:359
  41.8 1.6 %collective-permute-start.1 = (s16[16,1152]{1,0:T(8,128)(2,1)S(1)}, s16[16,1152]{1,0:T(8,128)(2,1)S(1)}, u32[]{:S(2)}, u32[]{:S(2)}) collective-permute-start(s16[16,1152]{1,0:T(8,128)(2,1)S(1)} %get-tuple-element.36), channel_id=1, source_target_pairs={{0,8},{8,16},{16,24},{24,32},{32,40},{40,48},{48,56},{56,64},{64,7... | collective-permute-start | bytes 110600 | tf_op jit(solution)/shard_map/ppermute | solution.py:382
  44.0 4.4 %collective-permute-done.1 = s16[16,1152]{1,0:T(8,128)(2,1)S(1)} collective-permute-done((s16[16,1152]{1,0:T(8,128)(2,1)S(1)}, s16[16,1152]{1,0:T(8,128)(2,1)S(1)}, u32[]{:S(2)}, u32[]{:S(2)}) %collective-permute-start.1) | collective-permute-done | bytes 36896 | tf_op jit(solution)/shard_map/ppermute | solution.py:382
  48.4 0.7 shard_map.85
  49.1 13.1 %all_to_all.42.got_ref = bf16[8,16,896]{2,1,0:T(8,128)(2,1)S(1)} all-to-all(bf16[8,16,896]{2,1,0:T(8,128)(2,1)S(1)} %get-tuple-element.41), channel_id=1, replica_groups=mesh['dp'=2,'section'=16,'tensor'=8] {'tensor'}, dimensions={0} | all-to-all | bytes 458752 | tf_op jit(solution)/shard_map/all_to_all | solution.py:359
  62.7 12.9 %all_to_all.43.got_ref = bf16[8,16,1024]{2,1,0:T(8,128)(2,1)S(1)} all-to-all(bf16[8,16,1024]{2,1,0:T(8,128)(2,1)S(1)} %shard_map.86), channel_id=1, replica_groups=mesh['dp'=2,'section'=16,'tensor'=8] {'tensor'}, dimensions={0} | all-to-all | bytes 524288 | tf_op jit(solution)/shard_map/all_to_all | solution.py:359
  75.6 0.6 shard_map.87
  76.3 1.6 %collective-permute-start.4 = (s16[16,1152]{1,0:T(8,128)(2,1)S(1)}, s16[16,1152]{1,0:T(8,128)(2,1)S(1)}, u32[]{:S(2)}, u32[]{:S(2)}) collective-permute-start(s16[16,1152]{1,0:T(8,128)(2,1)S(1)} %get-tuple-element.44), channel_id=1, source_target_pairs={{0,8},{8,16},{16,24},{24,32},{32,40},{40,48},{48,56},{56,64},{64,7... | collective-permute-start | bytes 110600 | tf_op jit(solution)/shard_map/ppermute | solution.py:382
  78.5 4.4 %collective-permute-done.4 = s16[16,1152]{1,0:T(8,128)(2,1)S(1)} collective-permute-done((s16[16,1152]{1,0:T(8,128)(2,1)S(1)}, s16[16,1152]{1,0:T(8,128)(2,1)S(1)}, u32[]{:S(2)}, u32[]{:S(2)}) %collective-permute-start.4) | collective-permute-done | bytes 36896 | tf_op jit(solution)/shard_map/ppermute | solution.py:382
  82.9 0.7 shard_map.88
  83.6 13.1 %all_to_all.44.got_ref = bf16[8,16,896]{2,1,0:T(8,128)(2,1)S(1)} all-to-all(bf16[8,16,896]{2,1,0:T(8,128)(2,1)S(1)} %get-tuple-element.48), channel_id=1, replica_groups=mesh['dp'=2,'section'=16,'tensor'=8] {'tensor'}, dimensions={0} | all-to-all | bytes 458752 | tf_op jit(solution)/shard_map/all_to_all | solution.py:359
  97.2 12.9 %all_to_all.45.got_ref = bf16[8,16,1024]{2,1,0:T(8,128)(2,1)S(1)} all-to-all(bf16[8,16,1024]{2,1,0:T(8,128)(2,1)S(1)} %shard_map.89), channel_id=1, replica_groups=mesh['dp'=2,'section'=16,'tensor'=8] {'tensor'}, dimensions={0} | all-to-all | bytes 524288 | tf_op jit(solution)/shard_map/all_to_all | solution.py:359
  110.1 0.6 shard_map.90
  110.9 1.3 collective-permute-start.7
  112.7 4.7 %collective-permute-done.7 = s16[16,1152]{1,0:T(8,128)(2,1)S(1)} collective-permute-done((s16[16,1152]{1,0:T(8,128)(2,1)S(1)}, s16[16,1152]{1,0:T(8,128)(2,1)S(1)}, u32[]{:S(2)}, u32[]{:S(2)}) %collective-permute-start.7) | collective-permute-done | bytes 36896 | tf_op jit(solution)/shard_map/ppermute | solution.py:382
  117.4 0.7 shard_map.91
  118.1 12.8 %all_to_all.46.got_ref = bf16[8,16,896]{2,1,0:T(8,128)(2,1)S(1)} all-to-all(bf16[8,16,896]{2,1,0:T(8,128)(2,1)S(1)} %get-tuple-element.55), channel_id=1, replica_groups=mesh['dp'=2,'section'=16,'tensor'=8] {'tensor'}, dimensions={0} | all-to-all | bytes 458752 | tf_op jit(solution)/shard_map/all_to_all | solution.py:359
  131.5 11.5 %all_to_all.47.got_ref = bf16[8,16,512]{2,1,0:T(8,128)(2,1)S(1)} all-to-all(bf16[8,16,512]{2,1,0:T(8,128)(2,1)S(1)} %shard_map.92), channel_id=1, replica_groups=mesh['dp'=2,'section'=16,'tensor'=8] {'tensor'}, dimensions={0} | all-to-all | bytes 262144 | tf_op jit(solution)/shard_map/all_to_all | solution.py:359
  143.0 0.6 shard_map.93
  143.7 1.3 collective-permute-start.10
  144.9 5.3 %collective-permute-done.10 = s16[16,1152]{1,0:T(8,128)(2,1)S(1)} collective-permute-done((s16[16,1152]{1,0:T(8,128)(2,1)S(1)}, s16[16,1152]{1,0:T(8,128)(2,1)S(1)}, u32[]{:S(2)}, u32[]{:S(2)}) %collective-permute-start.10) | collective-permute-done | bytes 36896 | tf_op jit(solution)/shard_map/ppermute | solution.py:382
  150.3 0.9 shard_map.94
  (40 shorter events, 5.0 us)
Async XLA Ops:
  0.0 27.6 %copy-start.1 = (bf16[1,4,4,64,256]{4,3,2,1,0:T(8,128)(2,1)S(1)}, bf16[1,4,4,64,256]{4,3,2,1,0:T(8,128)(2,1)}, u32[]{:S(2)}) copy-start(bf16[1,4,4,64,256]{4,3,2,1,0:T(8,128)(2,1)} %cache_far.1) | copy-start | bytes 1572868
  0.0 41.1 %copy-start = (bf16[1,2,1024,1024]{3,2,1,0:T(8,128)(2,1)S(1)}, bf16[1,2,1024,1024]{3,2,1,0:T(8,128)(2,1)}, u32[]{:S(2)}) copy-start(bf16[1,2,1024,1024]{3,2,1,0:T(8,128)(2,1)} %weight_ref.7) | copy-start | bytes 12582916
  0.0 48.4 %slice-start = ((s8[5242880]{0:T(1024)(128)(4,1)}), s8[4194304]{0:T(1024)(128)(4,1)S(1)}, s32[]{:S(2)}) async-start(s8[5242880]{0:T(1024)(128)(4,1)} %bitcast.5), calls=%async_computation.8 | async-start | bytes 8388608
  2.3 46.1 %slice-start.1 = ((s8[5242880]{0:T(1024)(128)(4,1)}), s8[1048576]{0:T(1024)(128)(4,1)S(1)}, s32[]{:S(2)}) async-start(s8[5242880]{0:T(1024)(128)(4,1)} %bitcast.5), calls=%async_computation.9 | async-start | bytes 2097152
  41.7 6.6 %collective-permute-start = (s16[48,1024]{1,0:T(8,128)(2,1)S(1)}, s16[48,1024]{1,0:T(8,128)(2,1)S(1)}, u32[]{:S(2)}, u32[]{:S(2)}) collective-permute-start(s16[48,1024]{1,0:T(8,128)(2,1)S(1)} %get-tuple-element.35), channel_id=1, source_target_pairs={{0,8},{8,16},{16,24},{24,32},{32,40},{40,48},{48,56},{56,64},{64,7... | collective-permute-start | bytes 294920 | tf_op jit(solution)/shard_map/ppermute | solution.py:382
  41.8 6.5 %collective-permute-start.1 = (s16[16,1152]{1,0:T(8,128)(2,1)S(1)}, s16[16,1152]{1,0:T(8,128)(2,1)S(1)}, u32[]{:S(2)}, u32[]{:S(2)}) collective-permute-start(s16[16,1152]{1,0:T(8,128)(2,1)S(1)} %get-tuple-element.36), channel_id=1, source_target_pairs={{0,8},{8,16},{16,24},{24,32},{32,40},{40,48},{48,56},{56,64},{64,7... | collective-permute-start | bytes 110600 | tf_op jit(solution)/shard_map/ppermute | solution.py:382
  43.4 5.7 %collective-permute-start.2 = (bf16[8,16,512]{2,1,0:T(8,128)(2,1)S(1)}, bf16[8,16,512]{2,1,0:T(8,128)(2,1)S(1)}, u32[]{:S(2)}, u32[]{:S(2)}) collective-permute-start(bf16[8,16,512]{2,1,0:T(8,128)(2,1)S(1)} %get-tuple-element.40.refs_0_), channel_id=1, source_target_pairs={{0,1},{1,0},{2,3},{3,2},{4,5},{5,4},{6,7},{7,6},{8,9},{9,8},{10,11... | collective-permute-start | bytes 393224 | tf_op jit(solution)/shard_map/ppermute | solution.py:387
  76.2 6.6 %collective-permute-start.3 = (s16[48,1024]{1,0:T(8,128)(2,1)S(1)}, s16[48,1024]{1,0:T(8,128)(2,1)S(1)}, u32[]{:S(2)}, u32[]{:S(2)}) collective-permute-start(s16[48,1024]{1,0:T(8,128)(2,1)S(1)} %get-tuple-element.43), channel_id=1, source_target_pairs={{0,8},{8,16},{16,24},{24,32},{32,40},{40,48},{48,56},{56,64},{64,7... | collective-permute-start | bytes 294920 | tf_op jit(solution)/shard_map/ppermute | solution.py:382
  76.3 6.5 %collective-permute-start.4 = (s16[16,1152]{1,0:T(8,128)(2,1)S(1)}, s16[16,1152]{1,0:T(8,128)(2,1)S(1)}, u32[]{:S(2)}, u32[]{:S(2)}) collective-permute-start(s16[16,1152]{1,0:T(8,128)(2,1)S(1)} %get-tuple-element.44), channel_id=1, source_target_pairs={{0,8},{8,16},{16,24},{24,32},{32,40},{40,48},{48,56},{56,64},{64,7... | collective-permute-start | bytes 110600 | tf_op jit(solution)/shard_map/ppermute | solution.py:382
  77.9 5.7 %collective-permute-start.5 = (bf16[8,16,512]{2,1,0:T(8,128)(2,1)S(1)}, bf16[8,16,512]{2,1,0:T(8,128)(2,1)S(1)}, u32[]{:S(2)}, u32[]{:S(2)}) collective-permute-start(bf16[8,16,512]{2,1,0:T(8,128)(2,1)S(1)} %get-tuple-element.47.refs_0_), channel_id=1, source_target_pairs={{0,1},{1,0},{2,3},{3,2},{4,5},{5,4},{6,7},{7,6},{8,9},{9,8},{10,11... | collective-permute-start | bytes 393224 | tf_op jit(solution)/shard_map/ppermute | solution.py:387
  110.8 6.6 %collective-permute-start.6 = (s16[48,1024]{1,0:T(8,128)(2,1)S(1)}, s16[48,1024]{1,0:T(8,128)(2,1)S(1)}, u32[]{:S(2)}, u32[]{:S(2)}) collective-permute-start(s16[48,1024]{1,0:T(8,128)(2,1)S(1)} %get-tuple-element.50), channel_id=1, source_target_pairs={{0,8},{8,16},{16,24},{24,32},{32,40},{40,48},{48,56},{56,64},{64,7... | collective-permute-start | bytes 294920 | tf_op jit(solution)/shard_map/ppermute | solution.py:382
  110.9 6.5 %collective-permute-start.7 = (s16[16,1152]{1,0:T(8,128)(2,1)S(1)}, s16[16,1152]{1,0:T(8,128)(2,1)S(1)}, u32[]{:S(2)}, u32[]{:S(2)}) collective-permute-start(s16[16,1152]{1,0:T(8,128)(2,1)S(1)} %get-tuple-element.51), channel_id=1, source_target_pairs={{0,8},{8,16},{16,24},{24,32},{32,40},{40,48},{48,56},{56,64},{64,7... | collective-permute-start | bytes 110600 | tf_op jit(solution)/shard_map/ppermute | solution.py:382
  112.2 5.9 %collective-permute-start.8 = (bf16[8,16,512]{2,1,0:T(8,128)(2,1)S(1)}, bf16[8,16,512]{2,1,0:T(8,128)(2,1)S(1)}, u32[]{:S(2)}, u32[]{:S(2)}) collective-permute-start(bf16[8,16,512]{2,1,0:T(8,128)(2,1)S(1)} %get-tuple-element.54.refs_0_), channel_id=1, source_target_pairs={{0,1},{1,0},{2,3},{3,2},{4,5},{5,4},{6,7},{7,6},{8,9},{9,8},{10,11... | collective-permute-start | bytes 393224 | tf_op jit(solution)/shard_map/ppermute | solution.py:387
  143.6 6.6 %collective-permute-start.9 = (s16[48,1024]{1,0:T(8,128)(2,1)S(1)}, s16[48,1024]{1,0:T(8,128)(2,1)S(1)}, u32[]{:S(2)}, u32[]{:S(2)}) collective-permute-start(s16[48,1024]{1,0:T(8,128)(2,1)S(1)} %get-tuple-element.57), channel_id=1, source_target_pairs={{0,8},{8,16},{16,24},{24,32},{32,40},{40,48},{48,56},{56,64},{64,7... | collective-permute-start | bytes 294920 | tf_op jit(solution)/shard_map/ppermute | solution.py:382
  143.7 6.5 %collective-permute-start.10 = (s16[16,1152]{1,0:T(8,128)(2,1)S(1)}, s16[16,1152]{1,0:T(8,128)(2,1)S(1)}, u32[]{:S(2)}, u32[]{:S(2)}) collective-permute-start(s16[16,1152]{1,0:T(8,128)(2,1)S(1)} %get-tuple-element.58), channel_id=1, source_target_pairs={{0,8},{8,16},{16,24},{24,32},{32,40},{40,48},{48,56},{56,64},{64,7... | collective-permute-start | bytes 110600 | tf_op jit(solution)/shard_map/ppermute | solution.py:382
